TPU v7x, 32 devices: a whole 2x2x4 slice. The times are simulated.
32 devices in a mesh: row: 4 (over z), col: 4 (over y, x), pan: 2 (over core).
Axes of the slice: x: 2, y: 2, z: 4, core: 2. Of those that a mesh axis runs over, the one named last changes fastest.
Arguments:
- plan_values: bfloat16 [4096, 32, 256], P('row', 'col', 'pan'), may hold values from 0.099609375 to 1
- plan_blocks: int32 [4, 32], P('row', 'col'), may hold values from 0 to 31, as said below
- first_values: bfloat16 [16, 3, 256, 256], P('row'), may hold values from -0.21875 to 0.21875
- first_blocks: int32 [16, 3], P('row'), may hold values from 0 to 3, as said below
- second_values: bfloat16 [32, 6, 256, 256], P('col', None, None, 'pan'), may hold values from -0.15625 to 0.15625
- second_blocks: int32 [32, 6], P('col'), may hold values from 0 to 7, as said below
- weight_first: float32 [4096], P('row'), may hold values from 0.5 to 2
- weight_second: float32 [32, 256], P('col', 'pan'), may hold values from 0.5 to 2
- offset_first: float32 [4096], P('row'), may hold values from -3 to 3
- offset_second: float32 [32, 256], P('col', 'pan'), may hold values from -3 to 3
Outputs:
- new_plan: bfloat16 [4096, 32, 256], P('row', 'col', 'pan')
- scale_first: float32 [4096], P('row')
- scale_second: float32 [32, 256], P('col', 'pan')
Inputs may be any that keep to these rules, and one draw needn't show every extreme that they name: `plan_blocks`: each entry is a slice-B block number; its column panel is the entry // 8. Within the 8 slots of one index of col (aligned groups of the second dimension) no column panel is named more than 2 times, and in every row panel one column panel is named exactly 2 times by every such group. `first_blocks`: block numbers within the row panel of the slice-A block; the 3 entries of a row are distinct. `second_blocks`: block numbers within the column panel of the slice-B block; the 6 entries of a row are distinct.
All inputs are finite; a program needn't handle non-finite values.
Results may differ from a plain program's by a relative error of at most 0.0087.
Values may be sent and summed in bfloat16 or wider, within the bound.
A program may use at most 128 MiB of HBM per device.

v0:
```python
import jax
import jax.numpy as jnp
from jax import lax
from jax.sharding import PartitionSpec as P

CAP = 2


def first_product(plan_values, first_values, first_blocks):
    tile_count = first_blocks.shape[0]
    block_size = first_values.shape[2]
    slot_count = plan_values.shape[1]
    half_width = plan_values.shape[2]
    row_tiles = plan_values.reshape(tile_count, block_size, slot_count * half_width)
    running = jnp.zeros(row_tiles.shape, jnp.float32)
    for neighbor in range(first_blocks.shape[1]):
        picked = jnp.take(row_tiles, first_blocks[:, neighbor], axis=0)
        running = running + jnp.einsum(
            "iab,ibn->ian", first_values[:, neighbor], picked, preferred_element_type=jnp.float32
        )
    return running.astype(jnp.bfloat16).reshape(tile_count * block_size, slot_count, half_width)


def dispatch(chooser, within_panel, product):
    outgoing = jnp.einsum(
        "dcs,rsh->dcrh", chooser.astype(jnp.bfloat16), product, preferred_element_type=jnp.float32
    ).astype(jnp.bfloat16)
    labels = jnp.sum(chooser.astype(jnp.int32) * (within_panel + 1)[None, None, :], axis=2) - 1
    return (outgoing, labels)


def second_product(dense_plan, second_values, second_blocks):
    blocks_here = second_blocks.shape[0]
    columns = jnp.arange(blocks_here)
    placer = (second_blocks[:, :, None] == columns[None, None, :]).astype(jnp.bfloat16)
    panel_matrix = jnp.einsum(
        "kqbh,kql->kblh", second_values, placer, preferred_element_type=jnp.float32
    ).astype(jnp.bfloat16)
    return jnp.einsum("rkb,kblh->rlh", dense_plan, panel_matrix, preferred_element_type=jnp.float32)


def local(
    plan_values,
    plan_blocks,
    first_values,
    first_blocks,
    second_values,
    second_blocks,
    weight_first,
    weight_second,
    offset_first,
    offset_second,
):
    col_count = lax.axis_size("col")
    blocks_here = second_blocks.shape[0]
    slot_count = plan_values.shape[1]
    block_size = first_values.shape[2]
    panel_rows = plan_values.shape[0]
    plan_width = float(slot_count * col_count * block_size)
    named_blocks = plan_blocks[0]
    target_panel = named_blocks // blocks_here
    within_panel = named_blocks % blocks_here
    same_panel = target_panel[:, None] == target_panel[None, :]
    earlier = jnp.arange(slot_count)[:, None] > jnp.arange(slot_count)[None, :]
    position = jnp.sum((same_panel & earlier).astype(jnp.int32), axis=1)
    chooser = (target_panel[None, None, :] == jnp.arange(col_count)[:, None, None]) & (
        position[None, None, :] == jnp.arange(CAP)[None, :, None]
    )
    product = first_product(plan_values, first_values, first_blocks)
    outgoing, labels = dispatch(chooser, within_panel, product)
    incoming, arrival_ids = (
        lax.all_to_all(outgoing, "col", split_axis=0, concat_axis=0, tiled=True),
        lax.all_to_all(labels, "col", split_axis=0, concat_axis=0, tiled=True),
    )
    item_rows = incoming.shape[2]
    arrivals = incoming.reshape(col_count * CAP, item_rows, incoming.shape[3])
    matcher = (arrival_ids.reshape(-1)[:, None] == jnp.arange(blocks_here)[None, :]).astype(
        jnp.bfloat16
    )
    dense_plan = jnp.einsum(
        "ik,irh->rkh", matcher, arrivals, preferred_element_type=jnp.float32
    ).astype(jnp.bfloat16)
    present = jnp.minimum(jnp.sum(matcher.astype(jnp.float32), axis=0), 1.0)
    gathered = lax.all_gather(dense_plan, "pan", axis=2, tiled=True)
    crossed = second_product(gathered, second_values, second_blocks)
    kernel_values = present[None, :, None] * jnp.exp(
        crossed - offset_first[:, None, None] - offset_second[None]
    )
    row_totals = lax.psum(jnp.sum(kernel_values, axis=(1, 2)), ("col", "pan"))
    scale_first = weight_first * plan_width / row_totals
    weighted = kernel_values * scale_first[:, None, None]
    colsum, counts = lax.psum((jnp.sum(weighted, axis=0), present * float(panel_rows)), "row")
    scale_second = weight_second * counts[:, None] / jnp.where(counts[:, None] > 0, colsum, 1.0)
    new_values = (weighted * scale_second[None]).astype(jnp.bfloat16)
    returned = jnp.einsum(
        "ik,rkh->irh", matcher, new_values, preferred_element_type=jnp.float32
    ).astype(jnp.bfloat16)
    returned = returned.reshape(col_count, CAP, item_rows, returned.shape[2])
    homeward = lax.all_to_all(returned, "col", split_axis=0, concat_axis=0, tiled=True)
    new_plan = jnp.einsum(
        "dcs,dcrh->rsh", chooser.astype(jnp.bfloat16), homeward, preferred_element_type=jnp.float32
    ).astype(jnp.bfloat16)
    return (new_plan, scale_first, scale_second)


def solution(mesh):
    return jax.shard_map(
        local,
        mesh=mesh,
        in_specs=(
            P("row", "col", "pan"),
            P("row", "col"),
            P("row", None, None, None),
            P("row", None),
            P("col", None, None, "pan"),
            P("col", None),
            P("row"),
            P("col", "pan"),
            P("row"),
            P("col", "pan"),
        ),
        out_specs=(P("row", "col", "pan"), P("row"), P("col", "pan")),
        check_vma=False,
    )
```

profile of v0, /device:TPU:0, one launch (start us, length us, event | category | flops | bytes accessed | tf_op | source)
XLA Modules:
  0.0 175.4 jit_solution(402431453181663967)
XLA Ops:
  7.2 0.0 copy-start
  7.2 0.8 fusion.57
  8.0 0.8 fusion.56
  8.8 0.2 convert_reduce_fusion.1
  9.0 0.2 fusion.45
  9.2 0.6 broadcast_add_fusion
  9.7 5.2 %all-to-all-start = ((s32[4,1,2]{2,1,0:T(1,128)}), s32[4,1,2]{2,1,0:T(1,128)S(1)}, u32[]{:S(2)}, u32[]{:S(2)}) async-start(s32[4,1,2]{2,1,0:T(1,128)} %bitcast.23), calls=%async_computation | async-start | bytes 4096 | tf_op jit(solution)/shard_map/all_to_all | solution.py:73
  14.9 1.0 slice_reduce_fusion.1
  16.0 4.2 %reshape.172 = bf16[4,256,1024]{2,1,0:T(8,128)(2,1)} reshape(bf16[1024,8,128]{2,1,0:T(8,128)(2,1)} %param.12) | data formatting | bytes 4194304 | tf_op jit(solution)/shard_map/reshape | solution.py:14
  20.2 3.6 %gather_fusion.2 = bf16[4,256,1024]{2,1,0:T(8,128)(2,1)} fusion(bf16[4,256,1024]{2,1,0:T(8,128)(2,1)} %reshape.172, s32[1024]{0:T(1024)S(1)} %pad_clamp_fusion), kind=kCustom, calls=%fused_computation.2.clone | custom fusion | bytes 4194320 | tf_op jit(solution)/shard_map/jit(_take)/gather | solution.py:17
  23.8 3.6 %gather_fusion.1 = bf16[4,256,1024]{2,1,0:T(8,128)(2,1)} fusion(bf16[4,256,1024]{2,1,0:T(8,128)(2,1)} %reshape.172, s32[1024]{0:T(1024)S(1)} %pad_clamp_fusion.1), kind=kCustom, calls=%fused_computation.1.clone | custom fusion | bytes 4194320 | tf_op jit(solution)/shard_map/jit(_take)/gather | solution.py:17
  27.4 3.6 %gather_fusion = bf16[4,256,1024]{2,1,0:T(8,128)(2,1)} fusion(bf16[4,256,1024]{2,1,0:T(8,128)(2,1)} %reshape.172, s32[1024]{0:T(1024)S(1)} %pad_clamp_fusion.2), kind=kCustom, calls=%fused_computation.clone | custom fusion | bytes 4194320 | tf_op jit(solution)/shard_map/jit(_take)/gather | solution.py:17
  31.0 0.0 copy-start.2
  31.0 0.0 copy-start.3
  31.0 2.8 %fusion.19 = f32[4,1024,256]{2,1,0:T(8,128)S(1)} fusion(bf16[4,256,1024]{2,1,0:T(8,128)(2,1)} %gather_fusion, pred[4]{0:T(512)(128)(4,1)S(1)} %compare_and_fusion.2, bf16[4,3,256,256]{3,2,1,0:T(8,128)(2,1)} %param.14), kind=kOutput, calls=%fused_computation.26 | convolution fusion | flops 537919488 | bytes 6815748 | tf_op jit(solution)/shard_map/iab,ibn->ian/dot_general | solution.py:18
  33.8 0.0 copy-done.2
  33.8 0.0 copy-done.3
  33.8 0.0 copy-start.1
  33.8 1.0 fusion.17
  34.9 0.5 copy-done.1
  35.4 2.7 %fusion.29 = bf16[4,256,1024]{1,2,0:T(8,128)(2,1)} fusion(bf16[4,256,1024]{2,1,0:T(8,128)(2,1)S(1)} %copy-done.1, pred[4]{0:T(512)(128)(4,1)S(1)} %get-tuple-element.17, f32[4,1024,256]{2,1,0:T(8,128)S(1)} %fusion.19, f32[4,1024,256]{2,1,0:T(8,128)S(1)} %fusion.17, bf16[4,3,256,256]{3,2,1,0:T(8,128)(2,1)S(1)} %copy-done.3), kind=kOutput, calls=%fused_computation.34 | convolution fusion | flops 541065216 | bytes 13107712 | tf_op jit(solution)/shard_map/iab,ibn->ian/dot_general | solution.py:18
  38.1 4.0 %copy.72 = bf16[4,256,1024]{2,1,0:T(8,128)(2,1)} copy(bf16[4,256,1024]{1,2,0:T(8,128)(2,1)} %fusion.29) | data formatting | bytes 4194304 | tf_op jit(solution)/shard_map/convert_element_type | solution.py:21
  42.1 2.2 %copy.98 = bf16[128,8,8,128]{3,2,1,0:T(8,128)(2,1)S(1)} copy(bf16[128,8,8,128]{3,1,2,0:T(8,128)(2,1)} %bitcast.95) | data formatting | bytes 4194304
  44.3 0.8 convolution_convert_fusion
  45.1 1.7 copy.74
  46.7 0.0 all-to-all-done
  46.7 4.4 %all-to-all-start.1 = ((bf16[4,2,1024,128]{3,2,1,0:T(8,128)(2,1)}), bf16[4,2,1024,128]{3,2,1,0:T(8,128)(2,1)}, u32[]{:S(2)}, u32[]{:S(2)}) async-start(bf16[4,2,1024,128]{3,2,1,0:T(8,128)(2,1)} %copy.74), calls=%async_computation.1 | async-start | bytes 4194304 | tf_op jit(solution)/shard_map/all_to_all | solution.py:72
  51.2 0.2 all-gather.2.cloned.1.call-start
  51.4 0.5 broadcast.271
  51.9 0.7 reduce.9
  52.6 0.1 eq.89
  52.7 23.5 %all-to-all-done.1 = bf16[4,2,1024,128]{3,2,1,0:T(8,128)(2,1)} async-done(((bf16[4,2,1024,128]{3,2,1,0:T(8,128)(2,1)}), bf16[4,2,1024,128]{3,2,1,0:T(8,128)(2,1)}, u32[]{:S(2)}, u32[]{:S(2)}) %all-to-all-start.1) | async-done | bytes 2097184 | tf_op jit(solution)/shard_map/all_to_all | solution.py:72
  76.1 4.3 %convert_bitcast_fusion.1 = bf16[1024,8,128]{2,1,0:T(8,128)(2,1)} fusion(bf16[8,1024,128]{2,1,0:T(8,128)(2,1)} %bitcast.9, s32[8]{0:T(128)S(1)} %eq.89), kind=kOutput, calls=%fused_computation.28 | convolution fusion | flops 17825856 | bytes 4194336 | tf_op jit(solution)/shard_map/ik,irh->rkh/dot_general | solution.py:80
  80.4 0.0 copy-start.8
  80.5 0.0 all-gather.2.cloned.1.call-update
  80.5 0.0 copy-done
  80.5 0.7 copy-done.8
  81.1 0.0 copy-start.6
  81.1 0.0 copy-start.7
  81.1 4.0 %convert_bitcast_fusion = bf16[8,256,8,128]{3,2,1,0:T(8,128)(2,1)} fusion(bf16[8,6,256,128]{3,2,1,0:T(8,128)(2,1)S(1)} %copy-done, s32[8,6]{1,0:T(8,128)S(1)} %copy-done.8), kind=kOutput, calls=%fused_computation.15 | convolution fusion | flops 27263360 | bytes 7340224 | tf_op jit(solution)/shard_map/kqbh,kql->kblh/dot_general | solution.py:36
  85.1 0.1 convert_reduce_fusion
  85.2 8.7 %all-gather.2.cloned.1.call-done = bf16[1024,8,256]{2,1,0:T(8,128)(2,1)} async-done(((bf16[1024,8,128]{2,1,0:T(8,128)(2,1)}), bf16[1024,8,256]{2,1,0:T(8,128)(2,1)}) %all-gather.2.cloned.1.call-update) | async-done | bytes 4194320 | tf_op jit(solution)/shard_map/all_gather | solution.py:84
  93.9 0.0 copy-done.6
  93.9 0.0 copy-done.7
  93.9 0.0 copy-start.9
  93.9 10.1 %fusion.11 = (f32[1024]{0:T(1024)S(1)}, f32[1024,8,128,1]{2,0,3,1:T(8,128)}) fusion(f32[8,128]{1,0:T(8,128)S(1)} %copy-done.6, f32[1024]{0:T(1024)S(1)} %copy-done.7, f32[8]{0:T(128)S(1)} %get-tuple-element.10, bf16[8,256,8,128]{3,2,1,0:T(8,128)(2,1)} %convert_bitcast_fusion, bf16[1024,8,256]{2,1,0:T(8,128)(2,1)} %all-gather.2.cloned.1.call-done), kind=kOutput, calls=%fused_computation.18 | convolution fusion | flops 4299160576 | bytes 12595232 | tf_op jit(solution)/shard_map/rkb,kblh->rlh/dot_general | solution.py:39
  104.0 14.3 %psum.21 = f32[1024]{0:T(1024)S(1)} all-reduce(f32[1024]{0:T(1024)S(1)} %get-tuple-element.13), channel_id=1, replica_groups=mesh['row'=4,'col'=4,'pan'=2] {'col','pan'}, use_global_device_ids=true, to_apply=%region_4.6 | all-reduce | flops 1024 | bytes 8192 | tf_op jit(solution)/shard_map/psum | solution.py:89
  118.3 0.0 copy-done.9
  118.3 0.0 copy-start.4
  118.3 0.0 copy-start.10
  118.3 3.3 %multiply_reduce_fusion = f32[8,128]{1,0:T(8,128)S(1)} fusion(f32[1024,8,128,1]{2,0,3,1:T(8,128)} %get-tuple-element.14, f32[1024]{0:T(1024)S(1)} %multiply_divide_fusion, f32[8,128]{1,0:T(8,128)S(1)} %copy-done.6, f32[1024]{0:T(1024)S(1)} %copy-done.7, f32[8]{0:T(128)S(1)} %get-tuple-element.10), kind=kLoop, calls=%fused_computation.17 | loop fusion | flops 5241856 | bytes 4210720 | tf_op jit(solution)/shard_map/reduce_sum | solution.py:92
  121.6 12.1 %all-reduce = (f32[8,128]{1,0:T(8,128)S(1)}, f32[8]{0:T(128)S(1)}) all-reduce(f32[8,128]{1,0:T(8,128)S(1)} %multiply_reduce_fusion, f32[8]{0:T(128)S(1)} %get-tuple-element.9), channel_id=1, replica_groups=mesh['row'=4,'col'=4,'pan'=2] {'row'}, use_global_device_ids=true, to_apply=%region_7.9 | all-reduce | flops 1032 | bytes 8256 | tf_op jit(solution)/shard_map/psum | solution.py:92
  133.7 0.0 copy-done.10
  133.7 0.1 select_divide_fusion
  133.8 0.0 copy-done.4
  133.8 0.0 copy-start.5
  133.8 3.9 %multiply_convert_fusion = bf16[1024,8,128]{2,0,1:T(8,128)(2,1)S(1)} fusion(f32[1024,8,128,1]{2,0,3,1:T(8,128)} %get-tuple-element.14, f32[8,128]{1,0:T(8,128)S(1)} %select_divide_fusion, f32[1024]{0:T(1024)S(1)} %multiply_divide_fusion, f32[8,128]{1,0:T(8,128)S(1)} %copy-done.6, f32[1024]{0:T(1024)S(1)} %copy-done.7, f32[8]{0:T(128)S(1)} %get-tuple-element.10), kind=kLoop, calls=%fused_computation.14 | loop fusion | flops 6291456 | bytes 6307872 | tf_op jit(solution)/shard_map/convert_element_type | solution.py:94
  137.6 0.0 copy-done.5
  137.6 1.3 fusion.26
  139.0 1.4 copy.81
  140.4 24.5 %all_to_all.16 = bf16[4,2,1024,128]{3,1,2,0:T(2,128)(2,1)S(1)} all-to-all(bf16[4,2,1024,128]{3,1,2,0:T(2,128)(2,1)S(1)} %copy.81), channel_id=1, replica_groups=mesh['row'=4,'col'=4,'pan'=2] {'col'}, dimensions={0} | all-to-all | bytes 4194304 | tf_op jit(solution)/shard_map/all_to_all | solution.py:99
  164.9 3.6 %fusion.32 = bf16[1024,8,128]{2,1,0:T(8,128)(2,1)} fusion(bf16[4,2,1024,128]{3,1,2,0:T(2,128)(2,1)S(1)} %all_to_all.16, pred[2,8]{1,0:T(4,128)(4,1)S(1)} %iota_compare_fusion.4, pred[4,8]{1,0:T(4,128)(4,1)S(1)} %iota_compare_fusion.3), kind=kOutput, calls=%fused_computation.35 | convolution fusion | flops 17825856 | bytes 4194352 | tf_op jit(solution)/shard_map/dcs,dcrh->rsh/dot_general | solution.py:100
  (13 shorter events, 0.1 us)
Async XLA Ops:
  7.2 73.3 %copy-start = (bf16[8,6,256,128]{3,2,1,0:T(8,128)(2,1)S(1)}, bf16[8,6,256,128]{3,2,1,0:T(8,128)(2,1)}, u32[]{:S(2)}) copy-start(bf16[8,6,256,128]{3,2,1,0:T(8,128)(2,1)} %param.16) | copy-start | bytes 9437188
  9.7 37.0 %all-to-all-start = ((s32[4,1,2]{2,1,0:T(1,128)}), s32[4,1,2]{2,1,0:T(1,128)S(1)}, u32[]{:S(2)}, u32[]{:S(2)}) async-start(s32[4,1,2]{2,1,0:T(1,128)} %bitcast.23), calls=%async_computation | async-start | bytes 4096 | tf_op jit(solution)/shard_map/all_to_all | solution.py:73
  31.0 2.8 %copy-start.2 = (bf16[4,256,1024]{2,1,0:T(8,128)(2,1)S(1)}, bf16[4,256,1024]{2,1,0:T(8,128)(2,1)}, u32[]{:S(2)}) copy-start(bf16[4,256,1024]{2,1,0:T(8,128)(2,1)} %gather_fusion.1) | copy-start | bytes 6291460
  31.0 2.8 %copy-start.3 = (bf16[4,3,256,256]{3,2,1,0:T(8,128)(2,1)S(1)}, bf16[4,3,256,256]{3,2,1,0:T(8,128)(2,1)}, u32[]{:S(2)}) copy-start(bf16[4,3,256,256]{3,2,1,0:T(8,128)(2,1)} %param.14) | copy-start | bytes 4718596
  33.8 1.6 copy-start.1
  46.7 29.4 %all-to-all-start.1 = ((bf16[4,2,1024,128]{3,2,1,0:T(8,128)(2,1)}), bf16[4,2,1024,128]{3,2,1,0:T(8,128)(2,1)}, u32[]{:S(2)}, u32[]{:S(2)}) async-start(bf16[4,2,1024,128]{3,2,1,0:T(8,128)(2,1)} %copy.74), calls=%async_computation.1 | async-start | bytes 4194304 | tf_op jit(solution)/shard_map/all_to_all | solution.py:72
  51.2 42.7 %all-gather.2.cloned.1.call-start = ((), (), s32[]{:S(2)}) async-start(), calls=%async_computation.3 | async-start | bytes 6291456 | tf_op jit(solution)/shard_map/all_gather | solution.py:84
  80.4 0.7 copy-start.8
  81.1 12.7 %copy-start.6 = (f32[8,128]{1,0:T(8,128)S(1)}, f32[8,128]{1,0:T(8,128)}, u32[]{:S(2)}) copy-start(f32[8,128]{1,0:T(8,128)} %param.21) | copy-start | bytes 12292
  81.1 12.7 %copy-start.7 = (f32[1024]{0:T(1024)S(1)}, f32[1024]{0:T(1024)}, u32[]{:S(2)}) copy-start(f32[1024]{0:T(1024)} %param.20) | copy-start | bytes 12292
  93.9 24.4 %copy-start.9 = (f32[1024]{0:T(1024)S(1)}, f32[1024]{0:T(1024)}, u32[]{:S(2)}) copy-start(f32[1024]{0:T(1024)} %param.18) | copy-start | bytes 12292
  118.3 15.5 %copy-start.4 = (f32[1024]{0:T(1024)}, f32[1024]{0:T(1024)S(1)}, u32[]{:S(2)}) copy-start(f32[1024]{0:T(1024)S(1)} %multiply_divide_fusion) | copy-start | bytes 12292
  118.3 15.4 %copy-start.10 = (f32[8,128]{1,0:T(8,128)S(1)}, f32[8,128]{1,0:T(8,128)}, u32[]{:S(2)}) copy-start(f32[8,128]{1,0:T(8,128)} %param.19) | copy-start | bytes 12292
  133.8 3.9 %copy-start.5 = (f32[8,128]{1,0:T(8,128)}, f32[8,128]{1,0:T(8,128)S(1)}, u32[]{:S(2)}) copy-start(f32[8,128]{1,0:T(8,128)S(1)} %select_divide_fusion) | copy-start | bytes 12292
Sparse Core Ops, SparseCore 0:
  80.6 13.2 all-gather.1
where the time goes:
time: 176 us; the launch traced here: 175 us
  blocking collectives  50.8 us (29%)
  waiting for transfers between devices  32.2 us (18%)
  matrix products  30.6 us (17%)
  local copies, waits for them, and re-layouts  27.1 us (15%)
  between operations  14.3 us (8%)
  other arithmetic  10.6 us (6%)
  starting transfers between devices  9.83 us (6%)
    all_to_all x1, blocking collectives, local(): lax.all_to_all(returned, 'col', split_axis=0, concat_axis=0, tiled=True)  24.5 us
    all_to_all x1, waiting for transfers between devices, local(): lax.all_to_all(outgoing, 'col', split_axis=0, concat_axis=0, tiled=True)  23.5 us
    psum x1, blocking collectives, local(): row_totals = lax.psum(jnp.sum(kernel_values, axis=(1, 2)), ('col', 'pan'))  14.3 us
    psum x1, blocking collectives, local(): lax.psum((jnp.sum(weighted, axis=0), present * float(panel_rows)), 'row')  12.1 us
    gather x3, local copies, waits for them, and re-layouts, first_product(): picked = jnp.take(row_tiles, first_blocks[:, neighbor], axis=0)  10.8 us
    dot_general x1, matrix products, second_product(): jnp.einsum('rkb,kblh->rlh', dense_plan, panel_matrix, preferred_element_t...  10.1 us
    all_gather x1, waiting for transfers between devices, local(): gathered = lax.all_gather(dense_plan, 'pan', axis=2, tiled=True)  8.69 us
    dot_general x3, matrix products, first_product(): jnp.einsum('iab,ibn->ian', first_values[:, neighbor], picked, preferred_e...  6.55 us
  transfers between devices with their start and end apart: 3, of which 2 were waited for; matrix products, arithmetic and copies ran while one was open for 21% of the time, Pallas kernels for 0%

commit v1 on v0

v1 whole, which is shorter than its diff:
```python
import functools

import jax
import jax.numpy as jnp
from jax import lax
from jax.experimental import pallas as pl
from jax.experimental.pallas import tpu as pltpu
from jax.sharding import PartitionSpec as P

CAP = 2
PAN = 2
GROUP = 8
MESH = pl.DeviceIdType.MESH
BF16_MAX = float(jnp.finfo(jnp.bfloat16).max)


def ranked_slot(read, slots, blocks_here, panel, rank):
    seen, found = jnp.int32(0), jnp.int32(-1)
    for s in range(slots):
        match = (lax.div(read(s), jnp.int32(blocks_here)) == panel).astype(jnp.int32)
        hit = match * (seen == rank).astype(jnp.int32)
        found = jnp.where(hit > 0, jnp.int32(s), found)
        seen = seen + match
    return found


def kernel(
    dims,
    tm_hbm,
    names_smem,
    names_vmem,
    first_hbm,
    near_smem,
    second_hbm,
    near_second_smem,
    weight_first,
    weight_second,
    offset_first,
    offset_second,
    out_ref,
    scale_first_ref,
    scale_second_ref,
    tm,
    first,
    second,
    product,
    outgoing,
    arrived,
    values,
    home,
    row_sums,
    col_sums,
    scales,
    names,
    row_scale,
    names_all,
    second_index,
    slot_of,
    label_of,
    present_of,
    item_of,
    local_sem,
    name_send,
    name_recv,
    out_send,
    out_recv,
    pan_send,
    pan_recv,
    back_send,
    back_recv,
    sum_send,
    sum_recv,
    col_send,
    col_recv,
    scale_send,
    scale_recv,
):
    C, R_AXIS, tiles, block, slots, half, blocks_here, near1, near2 = dims
    rows_total = tiles * block
    items = C * CAP
    row, me, pan = lax.axis_index("row"), lax.axis_index("col"), lax.axis_index("pan")
    other = 1 - pan

    def ahead(o):
        return lax.rem(me + o, C)

    def behind(o):
        return lax.rem(me - o + C, C)

    def row_ahead(o):
        return lax.rem(row + o, R_AXIS)

    def row_behind(o):
        return lax.rem(row - o + R_AXIS, R_AXIS)

    load_tm = pltpu.make_async_copy(tm_hbm, tm, local_sem.at[0])
    load_first = pltpu.make_async_copy(first_hbm, first, local_sem.at[1])
    load_second = pltpu.make_async_copy(
        second_hbm, second.at[pl.ds(0, blocks_here * near2)], local_sem.at[2]
    )
    load_tm.start()
    load_first.start()
    load_second.start()

    barrier = pltpu.get_barrier_semaphore()
    for oc in range(C):
        for oh in range(PAN):
            if oc or oh:
                pl.semaphore_signal(
                    barrier,
                    inc=1,
                    device_id=(row, ahead(oc), other if oh else pan),
                    device_id_type=MESH,
                )
    for o in range(1, R_AXIS):
        pl.semaphore_signal(
            barrier, inc=1, device_id=(row_ahead(o), me, pan), device_id_type=MESH
        )

    names[me] = jnp.zeros((8, 128), jnp.int32)
    names[me, 0:1, 0:slots] = names_vmem[...]
    second[blocks_here * near2] = jnp.zeros((block, half), jnp.bfloat16)
    row_sums[me * PAN + pan] = jnp.zeros((row_sums.shape[1], block), jnp.float32)

    def own_name(s):
        return names_smem[0, s]

    for d in range(C):
        for rank in range(CAP):
            slot_of[d * CAP + rank] = ranked_slot(own_name, slots, blocks_here, d, rank)
    for s in range(slots):
        panel = lax.div(own_name(s), jnp.int32(blocks_here))
        rank = jnp.int32(0)
        for t in range(s):
            rank = rank + (lax.div(own_name(t), jnp.int32(blocks_here)) == panel).astype(jnp.int32)
        item_of[0, s] = panel
        item_of[1, s] = jnp.minimum(rank, CAP - 1)
        item_of[2, s] = lax.rem(own_name(s), jnp.int32(blocks_here))

    pl.semaphore_wait(barrier, C * PAN - 1 + R_AXIS - 1)

    def send_names(o):
        return pltpu.make_async_remote_copy(
            src_ref=names.at[me],
            dst_ref=names.at[me],
            send_sem=name_send.at[o],
            recv_sem=name_recv.at[o],
            device_id=(row, ahead(o), pan),
            device_id_type=MESH,
        )

    def take_names(o):
        src = behind(o)
        return pltpu.make_async_remote_copy(
            src_ref=names.at[src],
            dst_ref=names.at[src],
            send_sem=name_send.at[o],
            recv_sem=name_recv.at[o],
            device_id=(row, src, pan),
            device_id_type=MESH,
        )

    for o in range(1, C):
        send_names(o).start()

    def dispatch(i, o):
        return pltpu.make_async_remote_copy(
            src_ref=outgoing.at[i, ahead(o)],
            dst_ref=arrived.at[pan, i, me],
            send_sem=out_send.at[i, o],
            recv_sem=out_recv.at[i, o],
            device_id=(row, ahead(o), pan),
            device_id_type=MESH,
        )

    def arrival(i, o):
        return pltpu.make_async_remote_copy(
            src_ref=outgoing.at[i, behind(o)],
            dst_ref=arrived.at[pan, i, behind(o)],
            send_sem=out_send.at[i, o],
            recv_sem=out_recv.at[i, o],
            device_id=(row, behind(o), pan),
            device_id_type=MESH,
        )

    def share(i, o):
        return pltpu.make_async_remote_copy(
            src_ref=arrived.at[pan, i, behind(o)],
            dst_ref=arrived.at[pan, i, behind(o)],
            send_sem=pan_send.at[i, o],
            recv_sem=pan_recv.at[i, o],
            device_id=(row, me, other),
            device_id_type=MESH,
        )

    def shared(i, o):
        return pltpu.make_async_remote_copy(
            src_ref=arrived.at[other, i, behind(o)],
            dst_ref=arrived.at[other, i, behind(o)],
            send_sem=pan_send.at[i, o],
            recv_sem=pan_recv.at[i, o],
            device_id=(row, me, other),
            device_id_type=MESH,
        )

    def give_back(i, o):
        return pltpu.make_async_remote_copy(
            src_ref=outgoing.at[i, ahead(o)],
            dst_ref=home.at[i, me],
            send_sem=back_send.at[i, o],
            recv_sem=back_recv.at[i, o],
            device_id=(row, ahead(o), pan),
            device_id_type=MESH,
        )

    def got_back(i, o):
        return pltpu.make_async_remote_copy(
            src_ref=outgoing.at[i, behind(o)],
            dst_ref=home.at[i, behind(o)],
            send_sem=back_send.at[i, o],
            recv_sem=back_recv.at[i, o],
            device_id=(row, behind(o), pan),
            device_id_type=MESH,
        )

    load_tm.wait()
    load_first.wait()

    def first_step(i, carry):
        left = jnp.concatenate([first[i, q] for q in range(near1)], axis=1)
        step = 2 * half
        for n in range(slots * half // step):
            right = jnp.concatenate(
                [tm[near_smem[i, q], :, n * step : (n + 1) * step] for q in range(near1)], axis=0
            )
            piece = jnp.dot(left, right, preferred_element_type=jnp.float32).astype(jnp.bfloat16)
            product[2 * n] = piece[:, :half]
            product[2 * n + 1] = piece[:, half:]
        for o in list(range(1, C)) + [0]:
            d = ahead(o)
            for rank in range(CAP):
                slot = slot_of[d * CAP + rank]
                piece = product[jnp.maximum(slot, 0)]
                keep = (slot >= 0).astype(jnp.float32).astype(jnp.bfloat16)
                piece = piece if items == slots else piece * keep
                if o:
                    outgoing[i, d, rank] = piece
                else:
                    arrived[pan, i, me, rank] = piece
            if o:
                dispatch(i, o).start()
            else:
                share(i, 0).start()
        return carry

    lax.fori_loop(0, tiles, first_step, 0)

    for o in range(1, C):
        take_names(o).wait_recv()
    copy_names = pltpu.make_async_copy(names, names_all, local_sem.at[3])
    copy_names.start()
    copy_names.wait()
    for src in range(C):
        for rank in range(CAP):
            read = lambda s: names_all[src, 0, s]
            slot = ranked_slot(read, slots, blocks_here, me, rank)
            name = lax.rem(read(jnp.maximum(slot, 0)), jnp.int32(blocks_here))
            label_of[src * CAP + rank] = jnp.where(slot >= 0, name, jnp.int32(-1))
    for l in range(blocks_here):
        hits = jnp.int32(0)
        for t in range(items):
            hits = hits + (label_of[t] == l).astype(jnp.int32)
        present_of[l] = jnp.minimum(hits, 1)

    def index_step(k, carry):
        for l in range(blocks_here):
            found = jnp.int32(blocks_here * near2)
            for q in range(near2):
                found = jnp.where(near_second_smem[k, q] == l, k * near2 + q, found)
            second_index[k, l] = found
        return carry

    lax.fori_loop(0, blocks_here, index_step, 0)
    load_second.wait()

    def spread(line):
        return jnp.transpose(jnp.broadcast_to(line, (half, block)))

    def second_step(i, carry):
        for o in range(1, C):
            arrival(i, o).wait_recv()
            share(i, o).start()
        for o in range(C):
            shared(i, o).wait_recv()
        at = pl.ds(pl.multiple_of(i * block, block), block)
        first_offset = spread(offset_first[pl.ds(i, 1), :])
        labels = [jnp.maximum(label_of[t], 0) for t in range(items)]
        total = jnp.zeros((block, half), jnp.float32)
        for pair in range(blocks_here // 2):
            crossed = None
            for start in range(0, items, GROUP):
                group = range(start, min(start + GROUP, items))
                left = jnp.concatenate(
                    [arrived[p, i, t // CAP, t % CAP] for t in group for p in range(PAN)], axis=1
                )
                right = jnp.concatenate(
                    [
                        jnp.concatenate(
                            [second[second_index[labels[t], 2 * pair + e]] for e in range(2)],
                            axis=1,
                        )
                        for t in group
                    ],
                    axis=0,
                )
                part = jnp.dot(left, right, preferred_element_type=jnp.float32)
                crossed = part if crossed is None else crossed + part
            for e in range(2):
                l = 2 * pair + e
                here = crossed[:, e * half : (e + 1) * half]
                seen = present_of[l].astype(jnp.float32)
                value = seen * jnp.exp(here - first_offset - offset_second[l : l + 1, :])
                values[l, at, :] = value
                total = total + value
        row_sums[me * PAN + pan, pl.ds(i, 1), :] = jnp.sum(
            jnp.transpose(total), axis=0, keepdims=True
        )
        for o in range(1, C):
            dispatch(i, o).wait_send()
        for o in list(range(1, C)) + [0]:
            d = ahead(o)
            for rank in range(CAP):
                label = jnp.maximum(label_of[d * CAP + rank], 0)
                value = jnp.minimum(values[label, at, :], BF16_MAX).astype(jnp.bfloat16)
                if o:
                    outgoing[i, d, rank] = value
                else:
                    home[i, me, rank] = value
            if o:
                give_back(i, o).start()
        return carry

    lax.fori_loop(0, tiles, second_step, 0)

    def sums_out(oc, oh):
        mine = me * PAN + pan
        return pltpu.make_async_remote_copy(
            src_ref=row_sums.at[mine],
            dst_ref=row_sums.at[mine],
            send_sem=sum_send.at[oc * PAN + oh],
            recv_sem=sum_recv.at[oc * PAN + oh],
            device_id=(row, ahead(oc), other if oh else pan),
            device_id_type=MESH,
        )

    def sums_in(oc, oh):
        theirs = behind(oc) * PAN + (other if oh else pan)
        return pltpu.make_async_remote_copy(
            src_ref=row_sums.at[theirs],
            dst_ref=row_sums.at[theirs],
            send_sem=sum_send.at[oc * PAN + oh],
            recv_sem=sum_recv.at[oc * PAN + oh],
            device_id=(row, behind(oc), other if oh else pan),
            device_id_type=MESH,
        )

    peers = [(oc, oh) for oc in range(C) for oh in range(PAN) if oc or oh]
    for oc, oh in peers:
        sums_out(oc, oh).start()
    for oc, oh in peers:
        sums_in(oc, oh).wait_recv()
    totals = row_sums[0, 0:tiles, :]
    for t in range(1, C * PAN):
        totals = totals + row_sums[t, 0:tiles, :]
    width = float(slots * C * block)
    scale_first_ref[...] = weight_first[...] * width / totals

    def col_step(i, sums):
        at = pl.ds(pl.multiple_of(i * block, block), block)
        scale = spread(scale_first_ref[pl.ds(i, 1), :])
        row_scale[at, :] = scale
        return tuple(
            sums[l] + jnp.sum(values[l, at, :] * scale, axis=0, keepdims=True)
            for l in range(blocks_here)
        )

    sums = lax.fori_loop(
        0, tiles, col_step, tuple(jnp.zeros((1, half), jnp.float32) for _ in range(blocks_here))
    )
    for l in range(blocks_here):
        col_sums[row, l : l + 1, :] = sums[l]
        col_sums[row, blocks_here + l : blocks_here + l + 1, :] = jnp.full(
            (1, half), present_of[l].astype(jnp.float32) * float(rows_total), jnp.float32
        )

    def cols_out(o):
        return pltpu.make_async_remote_copy(
            src_ref=col_sums.at[row],
            dst_ref=col_sums.at[row],
            send_sem=col_send.at[o],
            recv_sem=col_recv.at[o],
            device_id=(row_ahead(o), me, pan),
            device_id_type=MESH,
        )

    def cols_in(o):
        return pltpu.make_async_remote_copy(
            src_ref=col_sums.at[row_behind(o)],
            dst_ref=col_sums.at[row_behind(o)],
            send_sem=col_send.at[o],
            recv_sem=col_recv.at[o],
            device_id=(row_behind(o), me, pan),
            device_id_type=MESH,
        )

    for o in range(1, R_AXIS):
        cols_out(o).start()
    for o in range(1, R_AXIS):
        cols_in(o).wait_recv()
    both = col_sums[0]
    for t in range(1, R_AXIS):
        both = both + col_sums[t]
    colsum, counts = both[:blocks_here], both[blocks_here:]
    scale_second = weight_second[...] * counts / jnp.where(counts > 0, colsum, 1.0)
    scale_second_ref[...] = scale_second
    scales[me] = scale_second

    def scale_out(o):
        return pltpu.make_async_remote_copy(
            src_ref=scales.at[me],
            dst_ref=scales.at[me],
            send_sem=scale_send.at[o],
            recv_sem=scale_recv.at[o],
            device_id=(row, ahead(o), pan),
            device_id_type=MESH,
        )

    def scale_in(o):
        return pltpu.make_async_remote_copy(
            src_ref=scales.at[behind(o)],
            dst_ref=scales.at[behind(o)],
            send_sem=scale_send.at[o],
            recv_sem=scale_recv.at[o],
            device_id=(row, behind(o), pan),
            device_id_type=MESH,
        )

    for o in range(1, C):
        scale_out(o).start()
    for o in range(1, C):
        scale_in(o).wait_recv()

    def finish_waits(i, carry):
        for o in range(1, C):
            got_back(i, o).wait_recv()
        return carry

    lax.fori_loop(0, tiles, finish_waits, 0)

    def last_step(i, carry):
        at = pl.ds(pl.multiple_of(i * block, block), block)
        scale = row_scale[at, :]
        for s in range(slots):
            panel, rank, name = item_of[0, s], item_of[1, s], item_of[2, s]
            value = home[i, panel, rank].astype(jnp.float32) * scale
            value = value * scales[panel, pl.ds(name, 1), :]
            out_ref[at, s * half : (s + 1) * half] = value.astype(jnp.bfloat16)
        return carry

    lax.fori_loop(0, tiles, last_step, 0)

    def drain(i, carry):
        for o in range(C):
            share(i, o).wait_send()
        for o in range(1, C):
            give_back(i, o).wait_send()
        return carry

    lax.fori_loop(0, tiles, drain, 0)
    for o in range(1, C):
        send_names(o).wait_send()
        scale_out(o).wait_send()
    for oc, oh in peers:
        sums_out(oc, oh).wait_send()
    for o in range(1, R_AXIS):
        cols_out(o).wait_send()


def local(
    plan_values,
    plan_blocks,
    first_values,
    first_blocks,
    second_values,
    second_blocks,
    weight_first,
    weight_second,
    offset_first,
    offset_second,
):
    C, R_AXIS = lax.axis_size("col"), lax.axis_size("row")
    rows, slots, half = plan_values.shape
    tiles, near1, block, _ = first_values.shape
    blocks_here, near2 = second_blocks.shape
    dims = (C, R_AXIS, tiles, block, slots, half, blocks_here, near1, near2)
    sum_rows = -(-tiles // 8) * 8
    bf16, f32, i32 = jnp.bfloat16, jnp.float32, jnp.int32
    vmem, smem = pltpu.VMEM, pltpu.SMEM
    dma = pltpu.SemaphoreType.DMA
    in_vmem, in_smem = pl.BlockSpec(memory_space=vmem), pl.BlockSpec(memory_space=smem)
    anywhere = pl.BlockSpec(memory_space=pl.ANY)
    out, scale_first, scale_second = pl.pallas_call(
        functools.partial(kernel, dims),
        out_shape=(
            jax.ShapeDtypeStruct((rows, slots * half), bf16),
            jax.ShapeDtypeStruct((tiles, block), f32),
            jax.ShapeDtypeStruct((blocks_here, half), f32),
        ),
        in_specs=[
            anywhere,
            in_smem,
            in_vmem,
            anywhere,
            in_smem,
            anywhere,
            in_smem,
            in_vmem,
            in_vmem,
            in_vmem,
            in_vmem,
        ],
        out_specs=(in_vmem, in_vmem, in_vmem),
        scratch_shapes=[
            vmem((tiles, block, slots * half), bf16),
            vmem((tiles, near1, block, block), bf16),
            vmem((blocks_here * near2 + 1, block, half), bf16),
            vmem((slots, block, half), bf16),
            vmem((tiles, C, CAP, block, half), bf16),
            vmem((PAN, tiles, C, CAP, block, half), bf16),
            vmem((blocks_here, rows, half), f32),
            vmem((tiles, C, CAP, block, half), bf16),
            vmem((C * PAN, sum_rows, block), f32),
            vmem((R_AXIS, 2 * blocks_here, half), f32),
            vmem((C, blocks_here, half), f32),
            vmem((C, 8, 128), i32),
            vmem((rows, half), f32),
            smem((C, 8, 128), i32),
            smem((blocks_here, blocks_here), i32),
            smem((C * CAP,), i32),
            smem((C * CAP,), i32),
            smem((blocks_here,), i32),
            smem((3, slots), i32),
            dma((4,)),
            dma((C,)),
            dma((C,)),
            dma((tiles, C)),
            dma((tiles, C)),
            dma((tiles, C)),
            dma((tiles, C)),
            dma((tiles, C)),
            dma((tiles, C)),
            dma((C * PAN,)),
            dma((C * PAN,)),
            dma((R_AXIS,)),
            dma((R_AXIS,)),
            dma((C,)),
            dma((C,)),
        ],
        compiler_params=pltpu.CompilerParams(
            collective_id=0, has_side_effects=True, vmem_limit_bytes=60 * 1024 * 1024
        ),
        name="gromov_step",
    )(
        plan_values.reshape(tiles, block, slots * half),
        plan_blocks,
        plan_blocks,
        first_values,
        first_blocks,
        second_values.reshape(blocks_here * near2, block, half),
        second_blocks,
        weight_first.reshape(tiles, block),
        weight_second,
        offset_first.reshape(tiles, block),
        offset_second,
    )
    return out.reshape(rows, slots, half), scale_first.reshape(rows), scale_second


def solution(mesh):
    return jax.shard_map(
        local,
        mesh=mesh,
        in_specs=(
            P("row", "col", "pan"),
            P("row", "col"),
            P("row", None, None, None),
            P("row", None),
            P("col", None, None, "pan"),
            P("col", None),
            P("row"),
            P("col", "pan"),
            P("row"),
            P("col", "pan"),
        ),
        out_specs=(P("row", "col", "pan"), P("row"), P("col", "pan")),
        check_vma=False,
    )
```

time: 176 us -> 78.5 us (0.45)
  Pallas kernels: 0 us -> 66.1 us
  blocking collectives: 50.8 us -> 0 us
  waiting for transfers between devices: 32.2 us -> 0 us
  matrix products: 30.6 us -> 0 us
  local copies, waits for them, and re-layouts: 27.1 us -> 11.5 us
  between operations: 14.3 us -> 0.66 us
  other arithmetic: 10.6 us -> 0 us
  starting transfers between devices: 9.83 us -> 0 us
    pallas_call x0 -> x1, Pallas kernels: none -> 66.1 us  [local(): pl.pallas_call(functools.partial(kernel, dims), out_shape=(jax.ShapeDtype...]
    dot_general x9 -> x0, matrix products: 30.6 us -> none  [the longest x1 10.1 us: second_product(): jnp.einsum('rkb,kblh->rlh', dense_plan, panel_matrix, preferred_element_t...]
    psum x2 -> x0, blocking collectives: 26.4 us -> none  [the longest x1 14.3 us: local(): row_totals = lax.psum(jnp.sum(kernel_values, axis=(1, 2)), ('col', 'pan'))]
    all_to_all x1 -> x0, blocking collectives: 24.5 us -> none  [local(): lax.all_to_all(returned, 'col', split_axis=0, concat_axis=0, tiled=True)]
    all_to_all x2 -> x0, waiting for transfers between devices: 23.5 us -> none  [the longest x1 23.5 us: local(): lax.all_to_all(outgoing, 'col', split_axis=0, concat_axis=0, tiled=True)]
    gather x3 -> x0, local copies, waits for them, and re-layouts: 10.8 us -> none  [first_product(): picked = jnp.take(row_tiles, first_blocks[:, neighbor], axis=0)]
    all_to_all x2 -> x0, starting transfers between devices: 9.61 us -> none  [the longest x1 5.16 us: local(): lax.all_to_all(labels, 'col', split_axis=0, concat_axis=0, tiled=True)]
    all_gather x1 -> x0, waiting for transfers between devices: 8.69 us -> none  [local(): gathered = lax.all_gather(dense_plan, 'pan', axis=2, tiled=True)]
  transfers between devices with their start and end apart: 3 -> 0, of which waited for: 2 -> 0; matrix products, arithmetic and copies ran while one was open for 21% -> 0% of each run, Pallas kernels for 0% -> 0%
where the time goes in v1:
time: 78.5 us; the launch traced here: 78.2 us
  Pallas kernels  66.1 us (84%)
  local copies, waits for them, and re-layouts  11.5 us (15%)
    pallas_call x1, Pallas kernels, local(): pl.pallas_call(functools.partial(kernel, dims), out_shape=(jax.ShapeDtype...  66.1 us
    unnamed x7, local copies, waits for them, and re-layouts  4.74 us
    reshape x1, local copies, waits for them, and re-layouts, local(): plan_values.reshape(tiles, block, slots * half)  4.15 us

profile of v1, /device:TPU:0, one launch (start us, length us, event | category | flops | bytes accessed | tf_op | source)
XLA Modules:
  0.0 78.2 jit_solution(490673915898662862)
XLA Ops:
  0.6 1.3 %reshape.26.weight_first = f32[4,256]{1,0:T(4,128)} reshape(f32[1024]{0:T(1024)} %param.16) | data formatting | bytes 8192 | tf_op jit(solution)/shard_map/reshape | solution.py:581
  1.9 1.3 %reshape.27.offset_first = f32[4,256]{1,0:T(4,128)} reshape(f32[1024]{0:T(1024)} %param.18) | data formatting | bytes 8192 | tf_op jit(solution)/shard_map/reshape | solution.py:583
  3.2 4.2 %reshape.24.tm_hbm = bf16[4,256,1024]{2,1,0:T(8,128)(2,1)} reshape(bf16[1024,8,128]{2,1,0:T(8,128)(2,1)} %param.10) | data formatting | bytes 4194304 | tf_op jit(solution)/shard_map/reshape | solution.py:574
  7.4 66.1 %gromov_step.1 = (bf16[1024,1024]{1,0:T(8,128)(2,1)}, f32[4,256]{1,0:T(4,128)}, f32[8,128]{1,0:T(8,128)}) custom-call(bf16[4,256,1024]{2,1,0:T(8,128)(2,1)} %reshape.24.tm_hbm, s32[1,8]{1,0:T(1,128)} %names_vmem.1, s32[1,8]{1,0:T(1,128)} %names_vmem.1, bf16[4,3,256,256]{3,2,1,0:T(8,128)(2,1)} %first_hbm.1, s32[4,3]{1,0:T(4,128)} %near_smem.1, ...), custom_call_target="tpu_custom_call" | custom-call | tf_op jit(solution)/shard_map/gromov_step/pallas_call | solution.py:512
  73.4 0.0 copy-start.1
  73.4 0.0 copy-start
  73.5 3.5 %copy.13 = bf16[128,8,8,128]{3,2,1,0:T(8,128)(2,1)} copy(bf16[128,8,8,128]{3,1,2,0:T(8,128)(2,1)} %bitcast.7) | data formatting | bytes 4194304
  77.0 0.0 copy-done.1
  77.0 0.6 copy.14
  77.6 0.0 copy-done
  77.6 0.6 copy.16
Async XLA Ops:
  73.4 3.6 %copy-start.1 = (f32[4,256]{1,0:T(4,128)S(1)}, f32[4,256]{1,0:T(4,128)}, u32[]{:S(2)}) copy-start(f32[4,256]{1,0:T(4,128)} %get-tuple-element.7) | copy-start | bytes 12292
  73.4 4.2 %copy-start = (f32[8,128]{1,0:T(8,128)S(1)}, f32[8,128]{1,0:T(8,128)}, u32[]{:S(2)}) copy-start(f32[8,128]{1,0:T(8,128)} %get-tuple-element.14) | copy-start | bytes 12292

commit v2 on v1

--- a/solution.py
+++ b/solution.py
@@ -26,7 +26,7 @@
 
 def kernel(
     dims,
-    tm_hbm,
+    plan_hbm,
     names_smem,
     names_vmem,
     first_hbm,
@@ -40,6 +40,8 @@
     out_ref,
     scale_first_ref,
     scale_second_ref,
+    plan,
+    wide,
     tm,
     first,
     second,
@@ -47,7 +49,7 @@
     outgoing,
     arrived,
     values,
-    home,
+    finished,
     row_sums,
     col_sums,
     scales,
@@ -74,6 +76,9 @@
     col_recv,
     scale_send,
     scale_recv,
+    plan_sem,
+    done_sem,
+    *home,
 ):
     C, R_AXIS, tiles, block, slots, half, blocks_here, near1, near2 = dims
     rows_total = tiles * block
@@ -93,12 +98,17 @@
     def row_behind(o):
         return lax.rem(row - o + R_AXIS, R_AXIS)
 
-    load_tm = pltpu.make_async_copy(tm_hbm, tm, local_sem.at[0])
+    def load_plan(i):
+        return pltpu.make_async_copy(
+            plan_hbm.at[pl.ds(i * block, block)], plan.at[i], plan_sem.at[i]
+        )
+
     load_first = pltpu.make_async_copy(first_hbm, first, local_sem.at[1])
     load_second = pltpu.make_async_copy(
         second_hbm, second.at[pl.ds(0, blocks_here * near2)], local_sem.at[2]
     )
-    load_tm.start()
+    for i in range(tiles):
+        load_plan(i).start()
     load_first.start()
     load_second.start()
 
@@ -120,7 +130,6 @@
     names[me] = jnp.zeros((8, 128), jnp.int32)
     names[me, 0:1, 0:slots] = names_vmem[...]
     second[blocks_here * near2] = jnp.zeros((block, half), jnp.bfloat16)
-    row_sums[me * PAN + pan] = jnp.zeros((row_sums.shape[1], block), jnp.float32)
 
     def own_name(s):
         return names_smem[0, s]
@@ -137,6 +146,16 @@
         item_of[1, s] = jnp.minimum(rank, CAP - 1)
         item_of[2, s] = lax.rem(own_name(s), jnp.int32(blocks_here))
 
+    def relayout(i, carry):
+        load_plan(i).wait()
+        wide[...] = plan[i].astype(jnp.float32).reshape(block * slots, half)
+        for s in range(slots):
+            lane = wide[pl.ds(s, block, stride=slots), :]
+            tm[i, :, s * half : (s + 1) * half] = lane.astype(jnp.bfloat16)
+        return carry
+
+    lax.fori_loop(0, tiles, relayout, 0)
+
     pl.semaphore_wait(barrier, C * PAN - 1 + R_AXIS - 1)
 
     def send_names(o):
@@ -206,7 +225,7 @@
     def give_back(i, o):
         return pltpu.make_async_remote_copy(
             src_ref=outgoing.at[i, ahead(o)],
-            dst_ref=home.at[i, me],
+            dst_ref=home[i].at[me],
             send_sem=back_send.at[i, o],
             recv_sem=back_recv.at[i, o],
             device_id=(row, ahead(o), pan),
@@ -216,14 +235,13 @@
     def got_back(i, o):
         return pltpu.make_async_remote_copy(
             src_ref=outgoing.at[i, behind(o)],
-            dst_ref=home.at[i, behind(o)],
+            dst_ref=home[i].at[behind(o)],
             send_sem=back_send.at[i, o],
             recv_sem=back_recv.at[i, o],
             device_id=(row, behind(o), pan),
             device_id_type=MESH,
         )
 
-    load_tm.wait()
     load_first.wait()
 
     def first_step(i, carry):
@@ -286,14 +304,44 @@
     def spread(line):
         return jnp.transpose(jnp.broadcast_to(line, (half, block)))
 
-    def second_step(i, carry):
+    def sums_out(i, oc, oh):
+        mine = me * PAN + pan
+        return pltpu.make_async_remote_copy(
+            src_ref=row_sums.at[mine, i],
+            dst_ref=row_sums.at[mine, i],
+            send_sem=sum_send.at[i, oc * PAN + oh],
+            recv_sem=sum_recv.at[i, oc * PAN + oh],
+            device_id=(row, ahead(oc), other if oh else pan),
+            device_id_type=MESH,
+        )
+
+    def sums_in(i, oc, oh):
+        theirs = behind(oc) * PAN + (other if oh else pan)
+        return pltpu.make_async_remote_copy(
+            src_ref=row_sums.at[theirs, i],
+            dst_ref=row_sums.at[theirs, i],
+            send_sem=sum_send.at[i, oc * PAN + oh],
+            recv_sem=sum_recv.at[i, oc * PAN + oh],
+            device_id=(row, behind(oc), other if oh else pan),
+            device_id_type=MESH,
+        )
+
+    peers = [(oc, oh) for oc in range(C) for oh in range(PAN) if oc or oh]
+
+    def send_home(i):
+        for o in range(1, C):
+            give_back(i, o).start()
+
+    def second_step(i, carry, last=False):
         for o in range(1, C):
             arrival(i, o).wait_recv()
             share(i, o).start()
+        if last:
+            send_home(0)
         for o in range(C):
             shared(i, o).wait_recv()
         at = pl.ds(pl.multiple_of(i * block, block), block)
-        first_offset = spread(offset_first[pl.ds(i, 1), :])
+        first_offset = spread(offset_first[:, at])
         labels = [jnp.maximum(label_of[t], 0) for t in range(items)]
         total = jnp.zeros((block, half), jnp.float32)
         for pair in range(blocks_here // 2):
@@ -322,62 +370,41 @@
                 value = seen * jnp.exp(here - first_offset - offset_second[l : l + 1, :])
                 values[l, at, :] = value
                 total = total + value
-        row_sums[me * PAN + pan, pl.ds(i, 1), :] = jnp.sum(
-            jnp.transpose(total), axis=0, keepdims=True
-        )
+        row_sums[me * PAN + pan, i] = jnp.sum(jnp.transpose(total), axis=0, keepdims=True)
+        for oc, oh in peers:
+            sums_out(i, oc, oh).start()
         for o in range(1, C):
             dispatch(i, o).wait_send()
-        for o in list(range(1, C)) + [0]:
-            d = ahead(o)
+        for d in range(C):
             for rank in range(CAP):
                 label = jnp.maximum(label_of[d * CAP + rank], 0)
                 value = jnp.minimum(values[label, at, :], BF16_MAX).astype(jnp.bfloat16)
-                if o:
-                    outgoing[i, d, rank] = value
-                else:
-                    home[i, me, rank] = value
-            if o:
-                give_back(i, o).start()
+                outgoing[i, d, rank] = value
         return carry
 
-    lax.fori_loop(0, tiles, second_step, 0)
-
-    def sums_out(oc, oh):
-        mine = me * PAN + pan
-        return pltpu.make_async_remote_copy(
-            src_ref=row_sums.at[mine],
-            dst_ref=row_sums.at[mine],
-            send_sem=sum_send.at[oc * PAN + oh],
-            recv_sem=sum_recv.at[oc * PAN + oh],
-            device_id=(row, ahead(oc), other if oh else pan),
-            device_id_type=MESH,
-        )
-
-    def sums_in(oc, oh):
-        theirs = behind(oc) * PAN + (other if oh else pan)
-        return pltpu.make_async_remote_copy(
-            src_ref=row_sums.at[theirs],
-            dst_ref=row_sums.at[theirs],
-            send_sem=sum_send.at[oc * PAN + oh],
-            recv_sem=sum_recv.at[oc * PAN + oh],
-            device_id=(row, behind(oc), other if oh else pan),
-            device_id_type=MESH,
-        )
-
-    peers = [(oc, oh) for oc in range(C) for oh in range(PAN) if oc or oh]
-    for oc, oh in peers:
-        sums_out(oc, oh).start()
-    for oc, oh in peers:
-        sums_in(oc, oh).wait_recv()
-    totals = row_sums[0, 0:tiles, :]
-    for t in range(1, C * PAN):
-        totals = totals + row_sums[t, 0:tiles, :]
+    lax.fori_loop(0, tiles - 1, second_step, 0)
+    second_step(tiles - 1, 0, last=True)
+    held = list(range(1, tiles))
+
+    def release():
+        if held:
+            send_home(held.pop(0))
+
+    release()
+    for i in range(tiles):
+        for oc, oh in peers:
+            sums_in(i, oc, oh).wait_recv()
     width = float(slots * C * block)
-    scale_first_ref[...] = weight_first[...] * width / totals
+    for i in range(tiles):
+        part = slice(i * block, (i + 1) * block)
+        totals = row_sums[0, i]
+        for t in range(1, C * PAN):
+            totals = totals + row_sums[t, i]
+        scale_first_ref[:, part] = weight_first[:, part] * width / totals
 
     def col_step(i, sums):
         at = pl.ds(pl.multiple_of(i * block, block), block)
-        scale = spread(scale_first_ref[pl.ds(i, 1), :])
+        scale = spread(scale_first_ref[:, at])
         row_scale[at, :] = scale
         return tuple(
             sums[l] + jnp.sum(values[l, at, :] * scale, axis=0, keepdims=True)
@@ -415,6 +442,9 @@
 
     for o in range(1, R_AXIS):
         cols_out(o).start()
+    release()
+    for i in range(tiles):
+        home[i][me] = outgoing[i, me]
     for o in range(1, R_AXIS):
         cols_in(o).wait_recv()
     both = col_sums[0]
@@ -447,43 +477,46 @@
 
     for o in range(1, C):
         scale_out(o).start()
+    while held:
+        release()
     for o in range(1, C):
         scale_in(o).wait_recv()
 
-    def finish_waits(i, carry):
+    def store(i):
+        return pltpu.make_async_copy(
+            finished.at[i], out_ref.at[pl.ds(i * block, block)], done_sem.at[i]
+        )
+
+    for i in range(tiles):
         for o in range(1, C):
             got_back(i, o).wait_recv()
-        return carry
-
-    lax.fori_loop(0, tiles, finish_waits, 0)
-
-    def last_step(i, carry):
-        at = pl.ds(pl.multiple_of(i * block, block), block)
-        scale = row_scale[at, :]
+        scale = row_scale[i * block : (i + 1) * block, :]
         for s in range(slots):
             panel, rank, name = item_of[0, s], item_of[1, s], item_of[2, s]
-            value = home[i, panel, rank].astype(jnp.float32) * scale
+            value = home[i][panel, rank].astype(jnp.float32) * scale
             value = value * scales[panel, pl.ds(name, 1), :]
-            out_ref[at, s * half : (s + 1) * half] = value.astype(jnp.bfloat16)
-        return carry
-
-    lax.fori_loop(0, tiles, last_step, 0)
+            wide[pl.ds(s, block, stride=slots), :] = value
+        finished[i] = wide[...].reshape(block, slots, half).astype(jnp.bfloat16)
+        store(i).start()
 
     def drain(i, carry):
         for o in range(C):
             share(i, o).wait_send()
+        for oc, oh in peers:
+            sums_out(i, oc, oh).wait_send()
+        return carry
+
+    lax.fori_loop(0, tiles, drain, 0)
+    for i in range(tiles):
         for o in range(1, C):
             give_back(i, o).wait_send()
-        return carry
-
-    lax.fori_loop(0, tiles, drain, 0)
     for o in range(1, C):
         send_names(o).wait_send()
         scale_out(o).wait_send()
-    for oc, oh in peers:
-        sums_out(oc, oh).wait_send()
     for o in range(1, R_AXIS):
         cols_out(o).wait_send()
+    for i in range(tiles):
+        store(i).wait()
 
 
 def local(
@@ -503,7 +536,6 @@
     tiles, near1, block, _ = first_values.shape
     blocks_here, near2 = second_blocks.shape
     dims = (C, R_AXIS, tiles, block, slots, half, blocks_here, near1, near2)
-    sum_rows = -(-tiles // 8) * 8
     bf16, f32, i32 = jnp.bfloat16, jnp.float32, jnp.int32
     vmem, smem = pltpu.VMEM, pltpu.SMEM
     dma = pltpu.SemaphoreType.DMA
@@ -512,8 +544,8 @@
     out, scale_first, scale_second = pl.pallas_call(
         functools.partial(kernel, dims),
         out_shape=(
-            jax.ShapeDtypeStruct((rows, slots * half), bf16),
-            jax.ShapeDtypeStruct((tiles, block), f32),
+            jax.ShapeDtypeStruct((rows, slots, half), bf16),
+            jax.ShapeDtypeStruct((1, rows), f32),
             jax.ShapeDtypeStruct((blocks_here, half), f32),
         ),
         in_specs=[
@@ -529,8 +561,10 @@
             in_vmem,
             in_vmem,
         ],
-        out_specs=(in_vmem, in_vmem, in_vmem),
+        out_specs=(anywhere, in_vmem, in_vmem),
         scratch_shapes=[
+            vmem((tiles, block, slots, half), bf16),
+            vmem((block * slots, half), f32),
             vmem((tiles, block, slots * half), bf16),
             vmem((tiles, near1, block, block), bf16),
             vmem((blocks_here * near2 + 1, block, half), bf16),
@@ -538,8 +572,8 @@
             vmem((tiles, C, CAP, block, half), bf16),
             vmem((PAN, tiles, C, CAP, block, half), bf16),
             vmem((blocks_here, rows, half), f32),
-            vmem((tiles, C, CAP, block, half), bf16),
-            vmem((C * PAN, sum_rows, block), f32),
+            vmem((tiles, block, slots, half), bf16),
+            vmem((C * PAN, tiles, 1, block), f32),
             vmem((R_AXIS, 2 * blocks_here, half), f32),
             vmem((C, blocks_here, half), f32),
             vmem((C, 8, 128), i32),
@@ -559,31 +593,34 @@
             dma((tiles, C)),
             dma((tiles, C)),
             dma((tiles, C)),
-            dma((C * PAN,)),
-            dma((C * PAN,)),
+            dma((tiles, C * PAN)),
+            dma((tiles, C * PAN)),
             dma((R_AXIS,)),
             dma((R_AXIS,)),
             dma((C,)),
             dma((C,)),
-        ],
+            dma((tiles,)),
+            dma((tiles,)),
+        ]
+        + [vmem((C, CAP, block, half), bf16)] * tiles,
         compiler_params=pltpu.CompilerParams(
             collective_id=0, has_side_effects=True, vmem_limit_bytes=60 * 1024 * 1024
         ),
         name="gromov_step",
     )(
-        plan_values.reshape(tiles, block, slots * half),
+        plan_values,
         plan_blocks,
         plan_blocks,
         first_values,
         first_blocks,
         second_values.reshape(blocks_here * near2, block, half),
         second_blocks,
-        weight_first.reshape(tiles, block),
+        weight_first.reshape(1, rows),
         weight_second,
-        offset_first.reshape(tiles, block),
+        offset_first.reshape(1, rows),
         offset_second,
     )
-    return out.reshape(rows, slots, half), scale_first.reshape(rows), scale_second
+    return out, scale_first.reshape(rows), scale_second
 
 
 def solution(mesh):

time: 78.5 us -> 63.9 us (0.81)
  Pallas kernels: 66.1 us -> 58.8 us
  local copies, waits for them, and re-layouts: 11.5 us -> 4.24 us
    pallas_call x1, Pallas kernels: 66.1 us -> 58.8 us  [local(): pl.pallas_call(functools.partial(kernel, dims), out_shape=(jax.ShapeDtype...]
    reshape x3 -> x0, local copies, waits for them, and re-layouts: 6.72 us -> none  [the longest x1 4.15 us: local(): plan_values.reshape(tiles, block, slots * half)]
where the time goes in v2:
time: 63.9 us; the launch traced here: 63.7 us
  Pallas kernels  58.8 us (92%)
  local copies, waits for them, and re-layouts  4.24 us (7%)
  between operations  0.66 us (1%)
    pallas_call x1, Pallas kernels, local(): pl.pallas_call(functools.partial(kernel, dims), out_shape=(jax.ShapeDtype...  58.8 us
    unnamed x7, local copies, waits for them, and re-layouts  4.24 us

profile of v2, /device:TPU:0, one launch (start us, length us, event | category | flops | bytes accessed | tf_op | source)
XLA Modules:
  0.0 63.7 jit_solution(12240246415888683470)
XLA Ops:
  0.6 58.8 %gromov_step.1 = (bf16[1024,8,128]{2,1,0:T(8,128)(2,1)}, f32[1,1024]{1,0:T(1,128)}, f32[8,128]{1,0:T(8,128)}) custom-call(bf16[1024,8,128]{2,1,0:T(8,128)(2,1)} %plan_hbm.1, s32[1,8]{1,0:T(1,128)} %names_vmem.1, s32[1,8]{1,0:T(1,128)} %names_vmem.1, bf16[4,3,256,256]{3,2,1,0:T(8,128)(2,1)} %first_hbm.1, s32[4,3]{1,0:T(4,128)} %near_smem.1, ...), custom_call_target="tpu_custom_call" | custom-call | tf_op jit(solution)/shard_map/gromov_step/pallas_call | solution.py:544
  59.5 0.0 copy-start.1
  59.5 0.0 copy-start
  59.5 3.0 %copy.16 = bf16[1024,8,128]{2,1,0:T(8,128)(2,1)} copy(bf16[1024,8,128]{2,1,0:T(8,128)(2,1)} %get-tuple-element.12) | data formatting | bytes 4194304
  62.5 0.0 copy-done.1
  62.5 0.6 copy.17
  63.1 0.0 copy-done
  63.1 0.6 copy.18
Async XLA Ops:
  59.5 3.1 %copy-start.1 = (f32[1,1024]{1,0:T(1,128)S(1)}, f32[1,1024]{1,0:T(1,128)}, u32[]{:S(2)}) copy-start(f32[1,1024]{1,0:T(1,128)} %get-tuple-element.7) | copy-start | bytes 12292
  59.5 3.7 %copy-start = (f32[8,128]{1,0:T(8,128)S(1)}, f32[8,128]{1,0:T(8,128)}, u32[]{:S(2)}) copy-start(f32[8,128]{1,0:T(8,128)} %get-tuple-element.14) | copy-start | bytes 12292

commit v3 on v2

--- a/solution.py
+++ b/solution.py
@@ -86,11 +86,27 @@
     row, me, pan = lax.axis_index("row"), lax.axis_index("col"), lax.axis_index("pan")
     other = 1 - pan
 
+    bits = C.bit_length() - 1
+    paired = C == 1 << bits
+
+    def across(o):
+        shift = o
+        if bits > 1 and o % 4 in (1, 2):
+            shift = o + pan * (1 if o % 4 == 1 else -1)
+        result = 0
+        for b in range(bits):
+            result = result + lax.rem(lax.div(me, 1 << b) + lax.div(shift, 1 << b), 2) * (1 << b)
+        return result
+
     def ahead(o):
-        return lax.rem(me + o, C)
+        if o == 0:
+            return me
+        return across(o) if paired else lax.rem(me + o, C)
 
     def behind(o):
-        return lax.rem(me - o + C, C)
+        if o == 0:
+            return me
+        return across(o) if paired else lax.rem(me - o + C, C)
 
     def row_ahead(o):
         return lax.rem(row + o, R_AXIS)
@@ -332,12 +348,20 @@
         for o in range(1, C):
             give_back(i, o).start()
 
+    held = list(range(tiles - 1))
+
+    def release():
+        if held:
+            send_home(held.pop(0))
+
     def second_step(i, carry, last=False):
+        if last:
+            release()
         for o in range(1, C):
             arrival(i, o).wait_recv()
             share(i, o).start()
         if last:
-            send_home(0)
+            release()
         for o in range(C):
             shared(i, o).wait_recv()
         at = pl.ds(pl.multiple_of(i * block, block), block)
@@ -384,12 +408,7 @@
 
     lax.fori_loop(0, tiles - 1, second_step, 0)
     second_step(tiles - 1, 0, last=True)
-    held = list(range(1, tiles))
-
-    def release():
-        if held:
-            send_home(held.pop(0))
-
+    held.append(tiles - 1)
     release()
     for i in range(tiles):
         for oc, oh in peers:
@@ -517,6 +536,23 @@
         cols_out(o).wait_send()
     for i in range(tiles):
         store(i).wait()
+
+
+def hand_out(plan_in, first_in, second_in, plan_out, first_out, second_out, sems):
+    pieces = sems.shape[0] - 2
+    rows = plan_in.shape[0] // pieces
+    copies = [
+        pltpu.make_async_copy(
+            plan_in.at[pl.ds(i * rows, rows)], plan_out.at[pl.ds(i * rows, rows)], sems.at[i]
+        )
+        for i in range(pieces)
+    ]
+    copies.append(pltpu.make_async_copy(first_in, first_out, sems.at[pieces]))
+    copies.append(pltpu.make_async_copy(second_in, second_out, sems.at[pieces + 1]))
+    for copy in copies:
+        copy.start()
+    for copy in copies:
+        copy.wait()
 
 
 def local(
@@ -620,6 +656,15 @@
         offset_first.reshape(1, rows),
         offset_second,
     )
+    results = (out, scale_first, scale_second)
+    out, scale_first, scale_second = pl.pallas_call(
+        hand_out,
+        out_shape=tuple(jax.ShapeDtypeStruct(r.shape, r.dtype) for r in results),
+        in_specs=[anywhere] * 3,
+        out_specs=(anywhere,) * 3,
+        scratch_shapes=[dma((2 * tiles + 2,))],
+        name="hand_out",
+    )(*results)
     return out, scale_first.reshape(rows), scale_second
 
 

time: 63.9 us -> 126 us (1.97)
  Pallas kernels: 58.8 us -> 125 us
  local copies, waits for them, and re-layouts: 4.24 us -> 0 us
    pallas_call x0 -> x1, Pallas kernels: none -> 65 us  [local(): pl.pallas_call(hand_out, out_shape=tuple((jax.ShapeDtypeStruct(r.shape, r...]
    unnamed x7 -> x0, local copies, waits for them, and re-layouts: 4.24 us -> none
where the time goes in v3:
time: 126 us; the launch traced here: 125 us
  Pallas kernels  125 us (99%)
    pallas_call x1, Pallas kernels, local(): pl.pallas_call(hand_out, out_shape=tuple((jax.ShapeDtypeStruct(r.shape, r...  65 us
    pallas_call x1, Pallas kernels, local(): pl.pallas_call(functools.partial(kernel, dims), out_shape=(jax.ShapeDtype...  59.9 us

profile of v3, /device:TPU:0, one launch (start us, length us, event | category | flops | bytes accessed | tf_op | source)
XLA Modules:
  0.0 125.5 jit_solution(17076386566600179202)
XLA Ops:
  0.6 59.9 %gromov_step.1 = (bf16[1024,8,128]{2,1,0:T(8,128)(2,1)}, f32[1,1024]{1,0:T(1,128)}, f32[8,128]{1,0:T(8,128)}) custom-call(bf16[1024,8,128]{2,1,0:T(8,128)(2,1)} %plan_hbm.1, s32[1,8]{1,0:T(1,128)} %names_vmem.1, s32[1,8]{1,0:T(1,128)} %names_vmem.1, bf16[4,3,256,256]{3,2,1,0:T(8,128)(2,1)} %first_hbm.1, s32[4,3]{1,0:T(4,128)} %near_smem.1, ...), custom_call_target="tpu_custom_call" | custom-call | tf_op jit(solution)/shard_map/gromov_step/pallas_call | solution.py:580
  60.5 65.0 %hand_out.1 = (bf16[1024,8,128]{2,1,0:T(8,128)(2,1)}, f32[1,1024]{1,0:T(1,128)}, f32[8,128]{1,0:T(8,128)}) custom-call(bf16[1024,8,128]{2,1,0:T(8,128)(2,1)} %get-tuple-element.9.plan_in, f32[1,1024]{1,0:T(1,128)} %get-tuple-element.10.first_in, f32[8,128]{1,0:T(8,128)} %get-tuple-element.11.second_in), custom_call_target="tpu_custom_call" | custom-call | tf_op jit(solution)/shard_map/hand_out/pallas_call | solution.py:660

commit v4 on v2

--- a/solution.py
+++ b/solution.py
@@ -332,12 +332,28 @@
         for o in range(1, C):
             give_back(i, o).start()
 
-    def second_step(i, carry, last=False):
+    def forward(i):
         for o in range(1, C):
             arrival(i, o).wait_recv()
             share(i, o).start()
-        if last:
-            send_home(0)
+
+    held = list(range(tiles))
+
+    def release():
+        if held:
+            send_home(held.pop(0))
+
+    def stage(i):
+        at = pl.ds(pl.multiple_of(i * block, block), block)
+        for o in range(1, C):
+            dispatch(i, o).wait_send()
+        for d in range(C):
+            for rank in range(CAP):
+                label = jnp.maximum(label_of[d * CAP + rank], 0)
+                value = jnp.minimum(values[label, at, :], BF16_MAX).astype(jnp.bfloat16)
+                outgoing[i, d, rank] = value
+
+    def second_step(i, carry):
         for o in range(C):
             shared(i, o).wait_recv()
         at = pl.ds(pl.multiple_of(i * block, block), block)
@@ -373,24 +389,24 @@
         row_sums[me * PAN + pan, i] = jnp.sum(jnp.transpose(total), axis=0, keepdims=True)
         for oc, oh in peers:
             sums_out(i, oc, oh).start()
-        for o in range(1, C):
-            dispatch(i, o).wait_send()
-        for d in range(C):
-            for rank in range(CAP):
-                label = jnp.maximum(label_of[d * CAP + rank], 0)
-                value = jnp.minimum(values[label, at, :], BF16_MAX).astype(jnp.bfloat16)
-                outgoing[i, d, rank] = value
         return carry
 
-    lax.fori_loop(0, tiles - 1, second_step, 0)
-    second_step(tiles - 1, 0, last=True)
-    held = list(range(1, tiles))
-
-    def release():
-        if held:
-            send_home(held.pop(0))
-
+    def middle_step(i, carry):
+        second_step(i, 0)
+        forward(i + 1)
+        stage(i)
+        return carry
+
+    forward(0)
+    lax.fori_loop(0, tiles - 2, middle_step, 0)
+    second_step(tiles - 2, 0)
     release()
+    forward(tiles - 1)
+    stage(tiles - 2)
+    release()
+    second_step(tiles - 1, 0)
+    release()
+    stage(tiles - 1)
     for i in range(tiles):
         for oc, oh in peers:
             sums_in(i, oc, oh).wait_recv()
@@ -517,6 +533,12 @@
         cols_out(o).wait_send()
     for i in range(tiles):
         store(i).wait()
+
+
+def hand_out(plan_in, first_in, second_in, plan_out, first_out, second_out):
+    plan_out[...] = plan_in[...]
+    first_out[...] = first_in[...]
+    second_out[...] = second_in[...]
 
 
 def local(
@@ -620,6 +642,18 @@
         offset_first.reshape(1, rows),
         offset_second,
     )
+    by_tile = pl.BlockSpec((block, slots, half), lambda i: (i, 0, 0))
+    whole_first = pl.BlockSpec((1, rows), lambda i: (0, 0))
+    whole_second = pl.BlockSpec((blocks_here, half), lambda i: (0, 0))
+    results = (out, scale_first, scale_second)
+    out, scale_first, scale_second = pl.pallas_call(
+        hand_out,
+        out_shape=tuple(jax.ShapeDtypeStruct(r.shape, r.dtype) for r in results),
+        grid=(tiles,),
+        in_specs=[by_tile, whole_first, whole_second],
+        out_specs=(by_tile, whole_first, whole_second),
+        name="hand_out",
+    )(*results)
     return out, scale_first.reshape(rows), scale_second
 
 

time: 63.9 us -> 64.4 us (level)
  Pallas kernels: 58.8 us -> 63.6 us
  local copies, waits for them, and re-layouts: 4.24 us -> 0 us
    unnamed x7 -> x0, local copies, waits for them, and re-layouts: 4.24 us -> none
    pallas_call x0 -> x1, Pallas kernels: none -> 3.8 us  [local(): pl.pallas_call(hand_out, out_shape=tuple((jax.ShapeDtypeStruct(r.shape, r...]
    pallas_call x1, Pallas kernels: 58.8 us -> 59.8 us  [local(): pl.pallas_call(functools.partial(kernel, dims), out_shape=(jax.ShapeDtype...]
where the time goes in v4:
time: 64.4 us; the launch traced here: 64.2 us
  Pallas kernels  63.6 us (99%)
    pallas_call x1, Pallas kernels, local(): pl.pallas_call(functools.partial(kernel, dims), out_shape=(jax.ShapeDtype...  59.8 us
    pallas_call x1, Pallas kernels, local(): pl.pallas_call(hand_out, out_shape=tuple((jax.ShapeDtypeStruct(r.shape, r...  3.8 us

profile of v4, /device:TPU:0, one launch (start us, length us, event | category | flops | bytes accessed | tf_op | source)
XLA Modules:
  0.0 64.2 jit_solution(3501022187668674240)
XLA Ops:
  0.6 59.8 %gromov_step.1 = (bf16[1024,8,128]{2,1,0:T(8,128)(2,1)}, f32[1,1024]{1,0:T(1,128)}, f32[8,128]{1,0:T(8,128)}) custom-call(bf16[1024,8,128]{2,1,0:T(8,128)(2,1)} %plan_hbm.1, s32[1,8]{1,0:T(1,128)} %names_vmem.1, s32[1,8]{1,0:T(1,128)} %names_vmem.1, bf16[4,3,256,256]{3,2,1,0:T(8,128)(2,1)} %first_hbm.1, s32[4,3]{1,0:T(4,128)} %near_smem.1, ...), custom_call_target="tpu_custom_call" | custom-call | tf_op jit(solution)/shard_map/gromov_step/pallas_call | solution.py:566
  60.4 3.8 %hand_out.1 = (bf16[1024,8,128]{2,1,0:T(8,128)(2,1)}, f32[1,1024]{1,0:T(1,128)}, f32[8,128]{1,0:T(8,128)}) custom-call(bf16[1024,8,128]{2,1,0:T(8,128)(2,1)} %get-tuple-element.9.plan_in, f32[1,1024]{1,0:T(1,128)} %get-tuple-element.10.first_in, f32[8,128]{1,0:T(8,128)} %get-tuple-element.11.second_in), custom_call_target="tpu_custom_call" | custom-call | tf_op jit(solution)/shard_map/hand_out/pallas_call | solution.py:649

commit v5 on v4

--- a/solution.py
+++ b/solution.py
@@ -37,9 +37,10 @@
     weight_second,
     offset_first,
     offset_second,
-    out_ref,
+    home,
     scale_first_ref,
     scale_second_ref,
+    scales_ref,
     plan,
     wide,
     tm,
@@ -49,18 +50,15 @@
     outgoing,
     arrived,
     values,
-    finished,
     row_sums,
     col_sums,
     scales,
     names,
-    row_scale,
     names_all,
     second_index,
     slot_of,
     label_of,
     present_of,
-    item_of,
     local_sem,
     name_send,
     name_recv,
@@ -77,8 +75,8 @@
     scale_send,
     scale_recv,
     plan_sem,
+    first_sem,
     done_sem,
-    *home,
 ):
     C, R_AXIS, tiles, block, slots, half, blocks_here, near1, near2 = dims
     rows_total = tiles * block
@@ -103,14 +101,16 @@
             plan_hbm.at[pl.ds(i * block, block)], plan.at[i], plan_sem.at[i]
         )
 
-    load_first = pltpu.make_async_copy(first_hbm, first, local_sem.at[1])
+    def load_first(i):
+        return pltpu.make_async_copy(first_hbm.at[i], first.at[i], first_sem.at[i])
+
     load_second = pltpu.make_async_copy(
         second_hbm, second.at[pl.ds(0, blocks_here * near2)], local_sem.at[2]
     )
     for i in range(tiles):
         load_plan(i).start()
-    load_first.start()
-    load_second.start()
+    for i in range(tiles):
+        load_first(i).start()
 
     barrier = pltpu.get_barrier_semaphore()
     for oc in range(C):
@@ -137,15 +137,6 @@
     for d in range(C):
         for rank in range(CAP):
             slot_of[d * CAP + rank] = ranked_slot(own_name, slots, blocks_here, d, rank)
-    for s in range(slots):
-        panel = lax.div(own_name(s), jnp.int32(blocks_here))
-        rank = jnp.int32(0)
-        for t in range(s):
-            rank = rank + (lax.div(own_name(t), jnp.int32(blocks_here)) == panel).astype(jnp.int32)
-        item_of[0, s] = panel
-        item_of[1, s] = jnp.minimum(rank, CAP - 1)
-        item_of[2, s] = lax.rem(own_name(s), jnp.int32(blocks_here))
-
     def relayout(i, carry):
         load_plan(i).wait()
         wide[...] = plan[i].astype(jnp.float32).reshape(block * slots, half)
@@ -155,6 +146,7 @@
         return carry
 
     lax.fori_loop(0, tiles, relayout, 0)
+    load_second.start()
 
     pl.semaphore_wait(barrier, C * PAN - 1 + R_AXIS - 1)
 
@@ -225,7 +217,7 @@
     def give_back(i, o):
         return pltpu.make_async_remote_copy(
             src_ref=outgoing.at[i, ahead(o)],
-            dst_ref=home[i].at[me],
+            dst_ref=home.at[i, me],
             send_sem=back_send.at[i, o],
             recv_sem=back_recv.at[i, o],
             device_id=(row, ahead(o), pan),
@@ -235,16 +227,16 @@
     def got_back(i, o):
         return pltpu.make_async_remote_copy(
             src_ref=outgoing.at[i, behind(o)],
-            dst_ref=home[i].at[behind(o)],
+            dst_ref=home.at[i, behind(o)],
             send_sem=back_send.at[i, o],
             recv_sem=back_recv.at[i, o],
             device_id=(row, behind(o), pan),
             device_id_type=MESH,
         )
 
-    load_first.wait()
 
     def first_step(i, carry):
+        load_first(i).wait()
         left = jnp.concatenate([first[i, q] for q in range(near1)], axis=1)
         step = 2 * half
         for n in range(slots * half // step):
@@ -400,13 +392,18 @@
     forward(0)
     lax.fori_loop(0, tiles - 2, middle_step, 0)
     second_step(tiles - 2, 0)
+    forward(tiles - 1)
     release()
-    forward(tiles - 1)
     stage(tiles - 2)
-    release()
     second_step(tiles - 1, 0)
     release()
     stage(tiles - 1)
+
+    def keep(i):
+        return pltpu.make_async_copy(outgoing.at[i, me], home.at[i, me], done_sem.at[i])
+
+    for i in range(tiles):
+        keep(i).start()
     for i in range(tiles):
         for oc, oh in peers:
             sums_in(i, oc, oh).wait_recv()
@@ -421,7 +418,6 @@
     def col_step(i, sums):
         at = pl.ds(pl.multiple_of(i * block, block), block)
         scale = spread(scale_first_ref[:, at])
-        row_scale[at, :] = scale
         return tuple(
             sums[l] + jnp.sum(values[l, at, :] * scale, axis=0, keepdims=True)
             for l in range(blocks_here)
@@ -459,8 +455,6 @@
     for o in range(1, R_AXIS):
         cols_out(o).start()
     release()
-    for i in range(tiles):
-        home[i][me] = outgoing[i, me]
     for o in range(1, R_AXIS):
         cols_in(o).wait_recv()
     both = col_sums[0]
@@ -498,22 +492,10 @@
     for o in range(1, C):
         scale_in(o).wait_recv()
 
-    def store(i):
-        return pltpu.make_async_copy(
-            finished.at[i], out_ref.at[pl.ds(i * block, block)], done_sem.at[i]
-        )
-
+    scales_ref[...] = scales[...]
     for i in range(tiles):
         for o in range(1, C):
             got_back(i, o).wait_recv()
-        scale = row_scale[i * block : (i + 1) * block, :]
-        for s in range(slots):
-            panel, rank, name = item_of[0, s], item_of[1, s], item_of[2, s]
-            value = home[i][panel, rank].astype(jnp.float32) * scale
-            value = value * scales[panel, pl.ds(name, 1), :]
-            wide[pl.ds(s, block, stride=slots), :] = value
-        finished[i] = wide[...].reshape(block, slots, half).astype(jnp.bfloat16)
-        store(i).start()
 
     def drain(i, carry):
         for o in range(C):
@@ -532,11 +514,36 @@
     for o in range(1, R_AXIS):
         cols_out(o).wait_send()
     for i in range(tiles):
-        store(i).wait()
-
-
-def hand_out(plan_in, first_in, second_in, plan_out, first_out, second_out):
-    plan_out[...] = plan_in[...]
+        keep(i).wait()
+
+
+def hand_out(
+    blocks_here, names, home, first_in, second_in, scales, plan_out, first_out, second_out, wide, item_of
+):
+    _, _, _, rows, half = home.shape
+    slots = plan_out.shape[1]
+
+    def own_name(s):
+        return names[0, s]
+
+    @pl.when(pl.program_id(0) == 0)
+    def _():
+        for s in range(slots):
+            panel = lax.div(own_name(s), jnp.int32(blocks_here))
+            rank = jnp.int32(0)
+            for t in range(s):
+                rank = rank + (lax.div(own_name(t), jnp.int32(blocks_here)) == panel).astype(jnp.int32)
+            item_of[0, s] = panel
+            item_of[1, s] = jnp.minimum(rank, CAP - 1)
+            item_of[2, s] = lax.rem(own_name(s), jnp.int32(blocks_here))
+
+    scale = jnp.transpose(jnp.broadcast_to(first_in[...], (half, rows)))
+    for s in range(slots):
+        panel, rank, name = item_of[0, s], item_of[1, s], item_of[2, s]
+        value = home[0, panel, rank].astype(jnp.float32) * scale
+        value = value * scales[panel, pl.ds(name, 1), :]
+        wide[pl.ds(s, rows, stride=slots), :] = value
+    plan_out[...] = wide[...].reshape(rows, slots, half).astype(jnp.bfloat16)
     first_out[...] = first_in[...]
     second_out[...] = second_in[...]
 
@@ -563,12 +570,13 @@
     dma = pltpu.SemaphoreType.DMA
     in_vmem, in_smem = pl.BlockSpec(memory_space=vmem), pl.BlockSpec(memory_space=smem)
     anywhere = pl.BlockSpec(memory_space=pl.ANY)
-    out, scale_first, scale_second = pl.pallas_call(
+    home, scale_first, scale_second, scales = pl.pallas_call(
         functools.partial(kernel, dims),
         out_shape=(
-            jax.ShapeDtypeStruct((rows, slots, half), bf16),
+            jax.ShapeDtypeStruct((tiles, C, CAP, block, half), bf16),
             jax.ShapeDtypeStruct((1, rows), f32),
             jax.ShapeDtypeStruct((blocks_here, half), f32),
+            jax.ShapeDtypeStruct((C, blocks_here, half), f32),
         ),
         in_specs=[
             anywhere,
@@ -583,7 +591,7 @@
             in_vmem,
             in_vmem,
         ],
-        out_specs=(anywhere, in_vmem, in_vmem),
+        out_specs=(anywhere, in_vmem, in_vmem, in_vmem),
         scratch_shapes=[
             vmem((tiles, block, slots, half), bf16),
             vmem((block * slots, half), f32),
@@ -594,18 +602,15 @@
             vmem((tiles, C, CAP, block, half), bf16),
             vmem((PAN, tiles, C, CAP, block, half), bf16),
             vmem((blocks_here, rows, half), f32),
-            vmem((tiles, block, slots, half), bf16),
             vmem((C * PAN, tiles, 1, block), f32),
             vmem((R_AXIS, 2 * blocks_here, half), f32),
             vmem((C, blocks_here, half), f32),
             vmem((C, 8, 128), i32),
-            vmem((rows, half), f32),
             smem((C, 8, 128), i32),
             smem((blocks_here, blocks_here), i32),
             smem((C * CAP,), i32),
             smem((C * CAP,), i32),
             smem((blocks_here,), i32),
-            smem((3, slots), i32),
             dma((4,)),
             dma((C,)),
             dma((C,)),
@@ -623,8 +628,8 @@
             dma((C,)),
             dma((tiles,)),
             dma((tiles,)),
-        ]
-        + [vmem((C, CAP, block, half), bf16)] * tiles,
+            dma((tiles,)),
+        ],
         compiler_params=pltpu.CompilerParams(
             collective_id=0, has_side_effects=True, vmem_limit_bytes=60 * 1024 * 1024
         ),
@@ -642,18 +647,30 @@
         offset_first.reshape(1, rows),
         offset_second,
     )
-    by_tile = pl.BlockSpec((block, slots, half), lambda i: (i, 0, 0))
-    whole_first = pl.BlockSpec((1, rows), lambda i: (0, 0))
-    whole_second = pl.BlockSpec((blocks_here, half), lambda i: (0, 0))
-    results = (out, scale_first, scale_second)
+    step = block // 2
     out, scale_first, scale_second = pl.pallas_call(
-        hand_out,
-        out_shape=tuple(jax.ShapeDtypeStruct(r.shape, r.dtype) for r in results),
-        grid=(tiles,),
-        in_specs=[by_tile, whole_first, whole_second],
-        out_specs=(by_tile, whole_first, whole_second),
+        functools.partial(hand_out, blocks_here),
+        out_shape=(
+            jax.ShapeDtypeStruct((rows, slots, half), bf16),
+            jax.ShapeDtypeStruct((1, rows), f32),
+            jax.ShapeDtypeStruct((blocks_here, half), f32),
+        ),
+        grid=(2 * tiles,),
+        in_specs=[
+            in_smem,
+            pl.BlockSpec((1, C, CAP, step, half), lambda i: (i // 2, 0, 0, i % 2, 0)),
+            pl.BlockSpec((1, step), lambda i: (0, i)),
+            pl.BlockSpec((blocks_here, half), lambda i: (0, 0)),
+            pl.BlockSpec((C, blocks_here, half), lambda i: (0, 0, 0)),
+        ],
+        out_specs=(
+            pl.BlockSpec((step, slots, half), lambda i: (i, 0, 0)),
+            pl.BlockSpec((1, step), lambda i: (0, i)),
+            pl.BlockSpec((blocks_here, half), lambda i: (0, 0)),
+        ),
+        scratch_shapes=[vmem((step * slots, half), f32), smem((3, slots), i32)],
         name="hand_out",
-    )(*results)
+    )(plan_blocks, home, scale_first, scale_second, scales)
     return out, scale_first.reshape(rows), scale_second
 
 

time: 64.4 us -> 65.2 us (1.012)
  Pallas kernels: 63.6 us -> 64.3 us
    pallas_call x1, Pallas kernels: 3.8 us -> 6.34 us  [local(): pl.pallas_call(functools.partial(hand_out, blocks_here), out_shape=(jax.S...]
    pallas_call x1, Pallas kernels: 59.8 us -> 57.9 us  [local(): pl.pallas_call(functools.partial(kernel, dims), out_shape=(jax.ShapeDtype...]
where the time goes in v5:
time: 65.2 us; the launch traced here: 64.9 us
  Pallas kernels  64.3 us (99%)
    pallas_call x1, Pallas kernels, local(): pl.pallas_call(functools.partial(kernel, dims), out_shape=(jax.ShapeDtype...  57.9 us
    pallas_call x1, Pallas kernels, local(): pl.pallas_call(functools.partial(hand_out, blocks_here), out_shape=(jax.S...  6.34 us

profile of v5, /device:TPU:0, one launch (start us, length us, event | category | flops | bytes accessed | tf_op | source)
XLA Modules:
  0.0 64.9 jit_solution(2914379658590082467)
XLA Ops:
  0.6 57.9 %gromov_step.1 = (bf16[4,4,2,256,128]{4,3,2,1,0:T(8,128)(2,1)}, f32[1,1024]{1,0:T(1,128)}, f32[8,128]{1,0:T(8,128)}, f32[4,8,128]{2,1,0:T(8,128)}) custom-call(bf16[1024,8,128]{2,1,0:T(8,128)(2,1)} %plan_hbm.1, s32[1,8]{1,0:T(1,128)} %names.1, s32[1,8]{1,0:T(1,128)} %names.1, bf16[4,3,256,256]{3,2,1,0:T(8,128)(2,1)} %first_hbm.1, s32[4,3]{1,0:T(4,128)} %near_smem.1, ...), custom_call_target="tpu_custom_call" | custom-call | tf_op jit(solution)/shard_map/gromov_step/pallas_call | solution.py:573
  58.6 6.3 %hand_out.1 = (bf16[1024,8,128]{2,1,0:T(8,128)(2,1)}, f32[1,1024]{1,0:T(1,128)}, f32[8,128]{1,0:T(8,128)}) custom-call(s32[1,8]{1,0:T(1,128)} %names.1, bf16[4,4,2,256,128]{4,3,2,1,0:T(8,128)(2,1)} %get-tuple-element.10.home, f32[1,1024]{1,0:T(1,128)} %get-tuple-element.11.first_in, f32[8,128]{1,0:T(8,128)} %get-tuple-element.12.second_in, ...), custom_call_target="tpu_custom_call" | custom-call | tf_op jit(solution)/shard_map/hand_out/pallas_call | solution.py:651

commit v6 on v5

--- a/solution.py
+++ b/solution.py
@@ -42,7 +42,6 @@
     scale_second_ref,
     scales_ref,
     plan,
-    wide,
     tm,
     first,
     second,
@@ -139,10 +138,9 @@
             slot_of[d * CAP + rank] = ranked_slot(own_name, slots, blocks_here, d, rank)
     def relayout(i, carry):
         load_plan(i).wait()
-        wide[...] = plan[i].astype(jnp.float32).reshape(block * slots, half)
+        swapped = jnp.swapaxes(plan[i].astype(jnp.float32), 0, 1)
         for s in range(slots):
-            lane = wide[pl.ds(s, block, stride=slots), :]
-            tm[i, :, s * half : (s + 1) * half] = lane.astype(jnp.bfloat16)
+            tm[i, :, s * half : (s + 1) * half] = swapped[s].astype(jnp.bfloat16)
         return carry
 
     lax.fori_loop(0, tiles, relayout, 0)
@@ -518,7 +516,7 @@
 
 
 def hand_out(
-    blocks_here, names, home, first_in, second_in, scales, plan_out, first_out, second_out, wide, item_of
+    blocks_here, names, home, first_in, second_in, scales, plan_out, first_out, second_out, item_of
 ):
     _, _, _, rows, half = home.shape
     slots = plan_out.shape[1]
@@ -538,12 +536,12 @@
             item_of[2, s] = lax.rem(own_name(s), jnp.int32(blocks_here))
 
     scale = jnp.transpose(jnp.broadcast_to(first_in[...], (half, rows)))
+    pieces = []
     for s in range(slots):
         panel, rank, name = item_of[0, s], item_of[1, s], item_of[2, s]
         value = home[0, panel, rank].astype(jnp.float32) * scale
-        value = value * scales[panel, pl.ds(name, 1), :]
-        wide[pl.ds(s, rows, stride=slots), :] = value
-    plan_out[...] = wide[...].reshape(rows, slots, half).astype(jnp.bfloat16)
+        pieces.append(value * scales[panel, pl.ds(name, 1), :])
+    plan_out[...] = jnp.swapaxes(jnp.stack(pieces), 0, 1).astype(jnp.bfloat16)
     first_out[...] = first_in[...]
     second_out[...] = second_in[...]
 
@@ -594,7 +592,6 @@
         out_specs=(anywhere, in_vmem, in_vmem, in_vmem),
         scratch_shapes=[
             vmem((tiles, block, slots, half), bf16),
-            vmem((block * slots, half), f32),
             vmem((tiles, block, slots * half), bf16),
             vmem((tiles, near1, block, block), bf16),
             vmem((blocks_here * near2 + 1, block, half), bf16),
@@ -668,7 +665,7 @@
             pl.BlockSpec((1, step), lambda i: (0, i)),
             pl.BlockSpec((blocks_here, half), lambda i: (0, 0)),
         ),
-        scratch_shapes=[vmem((step * slots, half), f32), smem((3, slots), i32)],
+        scratch_shapes=[smem((3, slots), i32)],
         name="hand_out",
     )(plan_blocks, home, scale_first, scale_second, scales)
     return out, scale_first.reshape(rows), scale_second

time: 65.2 us -> 65.4 us (level)
  no operation moved by 1% of the time
where the time goes in v6:
time: 65.4 us; the launch traced here: 65.1 us
  Pallas kernels  64.4 us (98%)
    pallas_call x1, Pallas kernels, local(): pl.pallas_call(functools.partial(kernel, dims), out_shape=(jax.ShapeDtype...  57.9 us
    pallas_call x1, Pallas kernels, local(): pl.pallas_call(functools.partial(hand_out, blocks_here), out_shape=(jax.S...  6.5 us

profile of v6, /device:TPU:0, one launch (start us, length us, event | category | flops | bytes accessed | tf_op | source)
XLA Modules:
  0.0 65.1 jit_solution(11722705978232919137)
XLA Ops:
  0.6 57.9 %gromov_step.1 = (bf16[4,4,2,256,128]{4,3,2,1,0:T(8,128)(2,1)}, f32[1,1024]{1,0:T(1,128)}, f32[8,128]{1,0:T(8,128)}, f32[4,8,128]{2,1,0:T(8,128)}) custom-call(bf16[1024,8,128]{2,1,0:T(8,128)(2,1)} %plan_hbm.1, s32[1,8]{1,0:T(1,128)} %names.1, s32[1,8]{1,0:T(1,128)} %names.1, bf16[4,3,256,256]{3,2,1,0:T(8,128)(2,1)} %first_hbm.1, s32[4,3]{1,0:T(4,128)} %near_smem.1, ...), custom_call_target="tpu_custom_call" | custom-call | tf_op jit(solution)/shard_map/gromov_step/pallas_call | solution.py:571
  58.6 6.5 %hand_out.1 = (bf16[1024,8,128]{2,1,0:T(8,128)(2,1)}, f32[1,1024]{1,0:T(1,128)}, f32[8,128]{1,0:T(8,128)}) custom-call(s32[1,8]{1,0:T(1,128)} %names.1, bf16[4,4,2,256,128]{4,3,2,1,0:T(8,128)(2,1)} %get-tuple-element.10.home, f32[1,1024]{1,0:T(1,128)} %get-tuple-element.11.first_in, f32[8,128]{1,0:T(8,128)} %get-tuple-element.12.second_in, ...), custom_call_target="tpu_custom_call" | custom-call | tf_op jit(solution)/shard_map/hand_out/pallas_call | solution.py:648
